TPU v7x, 32 devices: a whole 2x2x4 slice. The times are simulated.
32 devices in a mesh: adapter: 16 (over z, y, core), tensor: 2 (over x).
Axes of the slice: x: 2, y: 2, z: 4, core: 2. Of those that a mesh axis runs over, the one named last changes fastest.
Arguments:
- residual_rows: bfloat16 [12288, 8192], P(('adapter', 'tensor')), may hold values from -6 to 6
- norm_gain_vector: bfloat16 [8192], replicated, may hold values from 0.099609375 to 1.8984375
- key_value_weight: bfloat16 [8192, 2048], P(None, 'tensor'), may hold values from -0.0625 to 0.0625
- adapter_down_weight: bfloat16 [128, 8192, 64], P('adapter', 'tensor'), may hold values from -0.0625 to 0.0625
- adapter_up_weight: bfloat16 [128, 64, 1024], P('adapter', None, 'tensor'), may hold values from -0.375 to 0.375
- request_adapter_index: int32 [3072, 1], P('adapter'), may hold values from 0 to 127, as said below
Outputs:
- projected: bfloat16 [12288, 2048], P('adapter', 'tensor')
Inputs may be any that keep to these rules, and one draw needn't show every extreme that they name: `request_adapter_index`: among the 192 requests of one index of adapter (aligned blocks of rows), no adapter is named more than 3 times and some adapter exactly 3 times; adapters a with the same a // 8 are named at most 12 times together, and some such set exactly 12 times.
All inputs are finite; a program needn't handle non-finite values.
Results may differ from a plain program's by a relative error of at most 0.0055.
Values may be sent and summed in bfloat16 or wider, within the bound.
No kernel may reach another device: no remote copies, remote signals or barrier semaphores. Data moves between devices by JAX's collectives and lax.ppermute only.
A program may use at most 128 MiB of HBM per device.

v0:
```python
import jax
import jax.numpy as jnp
from jax import lax
from jax.sharding import PartitionSpec as P

DRAFT = 4
MOST = 3


EPS = 1e-05
ADAPTER_SCALE = 2.0


def shrink_then_expand(received_rows, adapter_down_weight, adapter_up_weight):
    partial_value = jnp.einsum(
        "chje,hex->chjx", received_rows, adapter_down_weight, preferred_element_type=jnp.float32
    )
    shrunk_rows = lax.psum(partial_value, "tensor").astype(jnp.bfloat16)
    expanded_value = jnp.einsum(
        "wqlg,qgu->wqlu", shrunk_rows, adapter_up_weight, preferred_element_type=jnp.float32
    )
    return (expanded_value * ADAPTER_SCALE).astype(jnp.bfloat16)


def per_device(
    residual_rows,
    norm_gain_vector,
    key_value_weight,
    adapter_down_weight,
    adapter_up_weight,
    request_adapter_index,
):
    values = residual_rows.astype(jnp.float32)
    inverse = lax.rsqrt(jnp.mean(values * values, axis=-1, keepdims=True) + EPS)
    normed = (values * inverse * norm_gain_vector.astype(jnp.float32)).astype(jnp.bfloat16)
    tensor_count = lax.axis_size("tensor")
    tensor_index = lax.axis_index("tensor")
    adapter_count = lax.axis_size("adapter")
    model_width = normed.shape[1]
    share_width = model_width // tensor_count
    column_block_width = adapter_up_weight.shape[2]
    resident_adapters = adapter_down_weight.shape[0]
    capacity = MOST * DRAFT
    slot_count = resident_adapters * adapter_count * capacity
    gathered = lax.all_gather(normed, "tensor", axis=0, tiled=True)
    group_tokens = gathered.shape[0]
    columns = lax.dynamic_slice_in_dim(gathered, tensor_index * share_width, share_width, 1)
    request_ids = request_adapter_index[:, 0]
    request_count = request_ids.shape[0]
    positions = lax.broadcasted_iota(jnp.int32, (request_count, request_count), 0)
    earlier = lax.broadcasted_iota(jnp.int32, (request_count, request_count), 1) < positions
    same = request_ids[:, None] == request_ids[None, :]
    ranking = jnp.sum((same & earlier).astype(jnp.int32), axis=1)
    draft_steps = jnp.arange(DRAFT, dtype=jnp.int32)[None, :]
    padded = jnp.concatenate([columns, jnp.zeros((1, share_width), jnp.bfloat16)], axis=0)
    request_slot = request_ids * capacity + ranking * DRAFT
    token_slot = (request_slot[:, None] + draft_steps).reshape(-1)
    sources = jnp.full((slot_count,), group_tokens, jnp.int32)
    sources = sources.at[token_slot].set(jnp.arange(group_tokens, dtype=jnp.int32))
    outgoing = padded[sources].reshape(adapter_count, resident_adapters, capacity, share_width)
    correction = shrink_then_expand(
        lax.all_to_all(outgoing, "adapter", split_axis=0, concat_axis=0, tiled=True),
        adapter_down_weight,
        adapter_up_weight,
    )
    returned = lax.all_to_all(correction, "adapter", split_axis=0, concat_axis=0, tiled=True)
    token_delta = returned.reshape(slot_count, column_block_width)[token_slot]
    base = jnp.dot(gathered, key_value_weight, preferred_element_type=jnp.float32)
    base = base.reshape(group_tokens, 2, column_block_width)
    keys = base[:, 0, :]
    vals = base[:, 1, :] + token_delta.astype(jnp.float32)
    joined = jnp.stack([keys, vals], axis=1).astype(jnp.bfloat16)
    return joined.reshape(group_tokens, 2 * column_block_width)


def solution(mesh):
    in_specs = (
        P(("adapter", "tensor"), None),
        P(),
        P(None, "tensor"),
        P("adapter", "tensor", None),
        P("adapter", None, "tensor"),
        P("adapter", None),
    )
    out_specs = P("adapter", "tensor")
    return jax.shard_map(
        per_device, mesh=mesh, in_specs=in_specs, out_specs=out_specs, check_vma=False
    )
```

profile of v0, /device:TPU:9, one launch (start us, length us, event | category | flops | bytes accessed | tf_op | source)
XLA Modules:
  0.0 612.7 jit_solution(5750878687062369986)
XLA Ops:
  6.5 4.3 fusion
  11.2 4.7 fusion.2
  17.0 3.4 scatter_custom_fusion
  20.4 149.3 %all-gather.2.cloned.1.call-done = bf16[768,8192]{1,0:T(8,128)(2,1)} async-done(((bf16[384,8192]{1,0:T(8,128)(2,1)}), bf16[768,8192]{1,0:T(8,128)(2,1)}) %all-gather.2.cloned.1.call-update) | async-done | bytes 12582928 | tf_op jit(solution)/shard_map/all_gather | solution.py:45
  169.7 3.2 constant_dynamic-slice_fusion
  172.9 3.1 concatenate.3
  176.0 25.7 %gather_fusion = bf16[1536,4096]{1,0:T(8,128)(2,1)} fusion(bf16[769,4096]{1,0:T(8,128)(2,1)} %concatenate.3, s32[2048]{0:T(1024)S(1)} %pad_clamp_fusion), kind=kCustom, calls=%fused_computation | custom fusion | bytes 25171968 | tf_op jit(solution)/shard_map/gather | solution.py:60
  201.7 17.9 %reshape.71 = bf16[16,8,12,4096]{3,2,1,0:T(8,128)(2,1)} reshape(bf16[1536,4096]{1,0:T(8,128)(2,1)} %gather_fusion) | data formatting | bytes 25165824 | tf_op jit(solution)/shard_map/reshape | solution.py:60
  219.6 13.2 %copy.32 = bf16[16,8,12,4096]{3,1,2,0:T(8,128)(2,1)} copy(bf16[16,8,12,4096]{3,2,1,0:T(8,128)(2,1)} %reshape.71) | data formatting | bytes 25165824 | tf_op jit(solution)/shard_map/reshape | solution.py:60
  232.9 6.4 %all-to-all-start = ((bf16[16,8,12,4096]{3,1,2,0:T(8,128)(2,1)}), bf16[16,8,12,4096]{3,1,2,0:T(8,128)(2,1)}, u32[]{:S(2)}, u32[]{:S(2)}) async-start(bf16[16,8,12,4096]{3,1,2,0:T(8,128)(2,1)} %copy.32), calls=%async_computation | async-start | bytes 25165824 | tf_op jit(solution)/shard_map/all_to_all | solution.py:62
  239.2 270.1 %all-to-all-done = bf16[16,8,12,4096]{3,1,2,0:T(8,128)(2,1)} async-done(((bf16[16,8,12,4096]{3,1,2,0:T(8,128)(2,1)}), bf16[16,8,12,4096]{3,1,2,0:T(8,128)(2,1)}, u32[]{:S(2)}, u32[]{:S(2)}) %all-to-all-start) | async-done | bytes 12582944 | tf_op jit(solution)/shard_map/all_to_all | solution.py:62
  509.3 14.0 %fusion.8 = f32[16,8,12,64]{3,0,2,1:T(8,128)S(1)} fusion(bf16[8,4096,64]{1,2,0:T(8,128)(2,1)} %param.9, bf16[16,8,12,4096]{3,1,2,0:T(8,128)(2,1)} %all-to-all-done), kind=kOutput, calls=%fused_computation.17 | convolution fusion | flops 805306368 | bytes 17170432 | tf_op jit(solution)/shard_map/chje,hex->chjx/dot_general | solution.py:15
  523.3 20.2 %all-reduce.2 = bf16[16,8,12,64]{3,0,2,1:T(8,128)(2,1)S(1)} all-reduce(f32[16,8,12,64]{3,0,2,1:T(8,128)S(1)} %fusion.8), channel_id=1, replica_groups=mesh['adapter'=16,'tensor'=2] {'tensor'}, use_global_device_ids=true, to_apply=%region_3.0 | all-reduce | flops 98304 | bytes 589824 | tf_op jit(solution)/shard_map/psum | solution.py:18
  544.0 2.0 copy.34
  546.0 10.0 %all-to-all-start.1 = ((bf16[16,8,12,512]{3,1,2,0:T(8,128)(2,1)}), bf16[16,8,12,512]{3,1,2,0:T(8,128)(2,1)S(1)}, u32[]{:S(2)}, u32[]{:S(2)}) async-start(bf16[16,8,12,512]{3,1,2,0:T(8,128)(2,1)} %copy.34), calls=%async_computation.1 | async-start | bytes 3145728 | tf_op jit(solution)/shard_map/all_to_all | solution.py:66
  556.0 20.2 %fusion.19 = f32[768,1024]{1,0:T(8,128)} fusion(bf16[768,8192]{1,0:T(8,128)(2,1)} %all-gather.2.cloned.1.call-done, bf16[8192,1024]{1,0:T(8,128)(2,1)} %param.8), kind=kOutput, calls=%fused_computation.35 | convolution fusion | flops 12884901888 | bytes 32505856 | tf_op jit(solution)/shard_map/dot_general | solution.py:68
  576.2 5.6 reshape.70
  581.8 3.0 slice.13
  584.8 4.7 slice.14
  591.5 2.1 copy.35
  593.5 2.5 reshape.72
  596.0 2.7 gather_fusion.1
  598.7 1.7 fusion.6
  603.3 2.6 copy.37
  (27 shorter events, 6.9 us)
Async XLA Ops:
  6.5 536.9 %copy-start = (bf16[8,64,512]{2,1,0:T(8,128)(2,1)S(1)}, bf16[8,64,512]{2,1,0:T(8,128)(2,1)}, u32[]{:S(2)}) copy-start(bf16[8,64,512]{2,1,0:T(8,128)(2,1)} %param.10) | copy-start | bytes 1572868
  6.5 4.3 copy-start.2
  6.5 163.2 %all-gather.2.cloned.1.call-start = ((), (), s32[]{:S(2)}) async-start(), calls=%async_computation.2 | async-start | bytes 18874368 | tf_op jit(solution)/shard_map/all_gather | solution.py:45
  6.5 4.7 copy-start.1
  15.9 0.7 copy-start.3
  232.9 276.5 %all-to-all-start = ((bf16[16,8,12,4096]{3,1,2,0:T(8,128)(2,1)}), bf16[16,8,12,4096]{3,1,2,0:T(8,128)(2,1)}, u32[]{:S(2)}, u32[]{:S(2)}) async-start(bf16[16,8,12,4096]{3,1,2,0:T(8,128)(2,1)} %copy.32), calls=%async_computation | async-start | bytes 25165824 | tf_op jit(solution)/shard_map/all_to_all | solution.py:62
  546.0 45.5 %all-to-all-start.1 = ((bf16[16,8,12,512]{3,1,2,0:T(8,128)(2,1)}), bf16[16,8,12,512]{3,1,2,0:T(8,128)(2,1)S(1)}, u32[]{:S(2)}, u32[]{:S(2)}) async-start(bf16[16,8,12,512]{3,1,2,0:T(8,128)(2,1)} %copy.34), calls=%async_computation.1 | async-start | bytes 3145728 | tf_op jit(solution)/shard_map/all_to_all | solution.py:66
Sparse Core Ops, SparseCore 0:
  16.0 153.6 all-gather.1
where the time goes:
time: 615 us; the launch traced here: 613 us
  waiting for transfers between devices  420 us (68%)
  local copies, waits for them, and re-layouts  95.4 us (16%)
  matrix products  34.7 us (6%)
  blocking collectives  20.2 us (3%)
  starting transfers between devices  16.4 us (3%)
  between operations  13.5 us (2%)
  other arithmetic  12.2 us (2%)
    all_to_all x1, waiting for transfers between devices, per_device(): lax.all_to_all(outgoing, 'adapter', split_axis=0, concat_axis=0, tiled=True)  270 us
    all_gather x1, waiting for transfers between devices, per_device(): gathered = lax.all_gather(normed, 'tensor', axis=0, tiled=True)  149 us
    reshape x2, local copies, waits for them, and re-layouts, per_device(): padded[sources]  31.1 us
    gather x1, local copies, waits for them, and re-layouts, per_device(): padded[sources]  25.7 us
    dot_general x1, matrix products, per_device(): jnp.dot(gathered, key_value_weight, preferred_element_type=jnp.float32)  20.2 us
    psum x1, blocking collectives, shrink_then_expand(): shrunk_rows = lax.psum(partial_value, 'tensor').astype(jnp.bfloat16)  20.2 us
    dot_general x1, matrix products, shrink_then_expand(): jnp.einsum('chje,hex->chjx', received_rows, adapter_down_weight, preferre...  14 us
  transfers between devices with their start and end apart: 3, of which 3 were waited for; matrix products, arithmetic and copies ran while one was open for 6% of the time, Pallas kernels for 0%

commit v1 on v0

v1 whole, which is shorter than its diff:
```python
import jax
import jax.numpy as jnp
from jax import lax
from jax.sharding import PartitionSpec as P

DRAFT = 4
DEST = 12


EPS = 1e-05
ADAPTER_SCALE = 2.0


def chunk_bounds(width):
    first = max(width // 8, 128)
    second = first + max(width // 4, 128)
    return [(0, first), (first, second), (second, width)]


def onehot(row_of_column, rows):
    row = lax.broadcasted_iota(jnp.int32, (rows, row_of_column.shape[0]), 0)
    return (row == row_of_column[None, :]).astype(jnp.bfloat16)


def features(rows, start, width):
    return lax.dynamic_slice_in_dim(rows, start, width, 1)


def per_device(
    residual_rows,
    norm_gain_vector,
    key_value_weight,
    adapter_down_weight,
    adapter_up_weight,
    request_adapter_index,
):
    tensor_count = lax.axis_size("tensor")
    tensor_index = lax.axis_index("tensor")
    adapter_count = lax.axis_size("adapter")
    adapter_index = lax.axis_index("adapter")
    own_tokens, model_width = residual_rows.shape
    share_width = model_width // tensor_count
    column_block_width = adapter_up_weight.shape[2]
    resident_adapters = adapter_down_weight.shape[0]
    rank_width = adapter_down_weight.shape[2]
    holder_slots = DEST * DRAFT
    slot_count = adapter_count * holder_slots
    offsets = range(1, tensor_count)

    def to_offset(value, offset):
        pairs = [(i, (i + offset) % tensor_count) for i in range(tensor_count)]
        return lax.ppermute(value, "tensor", pairs)

    request_ids = request_adapter_index[:, 0]
    request_count = request_ids.shape[0]
    holder = request_ids // resident_adapters
    position = lax.broadcasted_iota(jnp.int32, (request_count, request_count), 0)
    earlier = lax.broadcasted_iota(jnp.int32, (request_count, request_count), 1) < position
    same = holder[:, None] == holder[None, :]
    ranking = jnp.sum((same & earlier).astype(jnp.int32), axis=1)
    request_slot = holder * DEST + ranking
    draft_steps = jnp.arange(DRAFT, dtype=jnp.int32)[None, :]
    token_slot = (request_slot[:, None] * DRAFT + draft_steps).reshape(-1)

    slot = lax.broadcasted_iota(jnp.int32, (adapter_count * DEST, request_count), 0)
    hit = slot == request_slot[None, :]
    local = request_ids - holder * resident_adapters
    slot_local = jnp.sum(jnp.where(hit, local[None, :] + 1, 0), axis=1) - 1
    told = lax.all_gather(slot_local.reshape(adapter_count, DEST), "adapter", axis=0)
    told = lax.dynamic_index_in_dim(told, adapter_index, 1, keepdims=False)
    slot_adapter = jnp.repeat(told.reshape(-1), DRAFT)

    def owner_slots(offset):
        owner = (tensor_index - offset) % tensor_count
        return lax.dynamic_slice_in_dim(token_slot, owner * own_tokens, own_tokens, 0)

    place = [onehot(owner_slots(offset), slot_count) for offset in range(tensor_count)]

    scaled = (
        residual_rows.astype(jnp.float32) * norm_gain_vector.astype(jnp.float32)
    ).astype(jnp.bfloat16)

    down = jnp.swapaxes(adapter_down_weight, 1, 2).reshape(resident_adapters * rank_width, share_width)
    partial_value = jnp.zeros((resident_adapters * rank_width, slot_count), jnp.float32)
    others = [jnp.zeros((own_tokens, 2 * column_block_width), jnp.float32) for _ in offsets]
    own_start = tensor_index * share_width
    for low, high in chunk_bounds(share_width):
        width = high - low
        outgoing = jnp.dot(
            place[0], features(scaled, own_start + low, width), preferred_element_type=jnp.float32
        )
        for offset in offsets:
            target = (tensor_index + offset) % tensor_count
            piece = to_offset(features(scaled, target * share_width + low, width), offset)
            outgoing += jnp.dot(place[offset], piece, preferred_element_type=jnp.float32)
            others[offset - 1] += jnp.dot(
                piece,
                lax.dynamic_slice_in_dim(key_value_weight, own_start + low, width, 0),
                preferred_element_type=jnp.float32,
            )
        outgoing = outgoing.astype(jnp.bfloat16).reshape(adapter_count, holder_slots, width)
        received = lax.all_to_all(outgoing, "adapter", split_axis=0, concat_axis=0, tiled=True)
        partial_value += lax.dot_general(
            down[:, low:high],
            received.reshape(slot_count, width),
            (((1,), (1,)), ((), ())),
            preferred_element_type=jnp.float32,
        )

    for offset in offsets:
        target = (tensor_index + offset) % tensor_count
        rest = jnp.concatenate(
            [features(scaled, (target + j) % tensor_count * share_width, share_width) for j in offsets],
            axis=1,
        )
        rest = to_offset(rest, offset)
        for j in offsets:
            weight_rows = lax.dynamic_slice_in_dim(
                key_value_weight, (tensor_index + j) % tensor_count * share_width, share_width, 0
            )
            others[offset - 1] += jnp.dot(
                rest[:, (j - 1) * share_width : j * share_width],
                weight_rows,
                preferred_element_type=jnp.float32,
            )
    own = jnp.dot(scaled, key_value_weight, preferred_element_type=jnp.float32)

    values = residual_rows.astype(jnp.float32)
    inverse = lax.rsqrt(jnp.mean(values * values, axis=-1) + EPS)
    inverse = [inverse] + [to_offset(inverse, offset) for offset in offsets]

    partial_value = partial_value.reshape(resident_adapters, rank_width, slot_count)
    mine = jnp.arange(resident_adapters, dtype=jnp.int32)[:, None, None] == slot_adapter[None, None, :]
    partial_value = jnp.sum(jnp.where(mine, partial_value, 0.0), axis=0)
    total = partial_value
    for offset in offsets:
        total += to_offset(partial_value, offset)
    shrunk = total.astype(jnp.bfloat16)
    spread = jnp.where(mine, shrunk[None], jnp.zeros((), jnp.bfloat16))
    correction = lax.dot_general(
        spread.reshape(resident_adapters * rank_width, slot_count),
        adapter_up_weight.reshape(resident_adapters * rank_width, column_block_width),
        (((0,), (0,)), ((), ())),
        preferred_element_type=jnp.float32,
    )
    correction = (correction * ADAPTER_SCALE).astype(jnp.bfloat16)
    returned = lax.all_to_all(
        correction.reshape(adapter_count, holder_slots, column_block_width),
        "adapter",
        split_axis=0,
        concat_axis=0,
        tiled=True,
    ).reshape(slot_count, column_block_width)

    result = jnp.zeros((own_tokens * tensor_count, 2 * column_block_width), jnp.bfloat16)
    for offset, base in enumerate([own] + others):
        delta = lax.dot_general(
            place[offset], returned, (((0,), (0,)), ((), ())), preferred_element_type=jnp.float32
        )
        keys = base[:, :column_block_width]
        vals = base[:, column_block_width:] + delta
        rows = (jnp.concatenate([keys, vals], axis=1) * inverse[offset][:, None]).astype(jnp.bfloat16)
        owner = (tensor_index - offset) % tensor_count
        result = lax.dynamic_update_slice_in_dim(result, rows, owner * own_tokens, 0)
    return result


def solution(mesh):
    in_specs = (
        P(("adapter", "tensor"), None),
        P(),
        P(None, "tensor"),
        P("adapter", "tensor", None),
        P("adapter", None, "tensor"),
        P("adapter", None),
    )
    out_specs = P("adapter", "tensor")
    return jax.shard_map(
        per_device, mesh=mesh, in_specs=in_specs, out_specs=out_specs, check_vma=False
    )
```

time: 615 us -> 269 us (0.44)
  waiting for transfers between devices: 420 us -> 121 us
  local copies, waits for them, and re-layouts: 95.4 us -> 13.4 us
  matrix products: 34.7 us -> 60.2 us
  starting transfers between devices: 16.4 us -> 32.8 us
  between operations: 13.5 us -> 0.32 us
  blocking collectives: 20.2 us -> 29.8 us
    all_to_all x1 -> x3, waiting for transfers between devices: 270 us -> 61.4 us  [per_device(): lax.all_to_all(outgoing, 'adapter', split_axis=0, concat_axis=0, tiled=True)]
    all_gather x1 -> x0, waiting for transfers between devices: 149 us -> none  [per_device(): gathered = lax.all_gather(normed, 'tensor', axis=0, tiled=True)]
    ppermute x0 -> x6, waiting for transfers between devices: none -> 56 us  [to_offset(): return lax.ppermute(value, 'tensor', pairs)]
    reshape x4 -> x1, local copies, waits for them, and re-layouts: 39.2 us -> 0.08 us  [per_device(): slot_adapter = jnp.repeat(told.reshape(-1), DRAFT)]
    all_gather x0 -> x1, blocking collectives: none -> 29.8 us  [per_device(): lax.all_gather(slot_local.reshape(adapter_count, DEST), 'adapter', axis=0)]
    gather x2 -> x0, local copies, waits for them, and re-layouts: 28.4 us -> none  [the longest x1 25.7 us: per_device(): padded[sources]]
    dot_general x3 -> x17, matrix products: 34.7 us -> 60.2 us  [the longest x1 12.3 us: per_device(): own = jnp.dot(scaled, key_value_weight, preferred_element_type=jnp.float32)]
    psum x1 -> x0, blocking collectives: 20.2 us -> none  [shrink_then_expand(): shrunk_rows = lax.psum(partial_value, 'tensor').astype(jnp.bfloat16)]
  transfers between devices with their start and end apart: 3 -> 10, of which waited for: 3 -> 5; matrix products, arithmetic and copies ran while one was open for 6% -> 25% of each run, Pallas kernels for 0% -> 0%
where the time goes in v1:
time: 269 us; the launch traced here: 268 us
  waiting for transfers between devices  121 us (45%)
  matrix products  60.2 us (22%)
  starting transfers between devices  32.8 us (12%)
  blocking collectives  29.8 us (11%)
  local copies, waits for them, and re-layouts  13.4 us (5%)
  other arithmetic  10.4 us (4%)
    all_to_all x3, waiting for transfers between devices, per_device(): lax.all_to_all(outgoing, 'adapter', split_axis=0, concat_axis=0, tiled=True)  61.4 us
    ppermute x6, waiting for transfers between devices, to_offset(): return lax.ppermute(value, 'tensor', pairs)  56 us
    all_gather x1, blocking collectives, per_device(): lax.all_gather(slot_local.reshape(adapter_count, DEST), 'adapter', axis=0)  29.8 us
    all_to_all x3, starting transfers between devices, per_device(): lax.all_to_all(outgoing, 'adapter', split_axis=0, concat_axis=0, tiled=True)  21.4 us
    dot_general x1, matrix products, per_device(): own = jnp.dot(scaled, key_value_weight, preferred_element_type=jnp.float32)  12.3 us
    dot_general x3, matrix products, per_device(): lax.dot_general(down[:, low:high], received.reshape(slot_count, width), (...  12.2 us
    dot_general x3, matrix products, per_device(): jnp.dot(piece, lax.dynamic_slice_in_dim(key_value_weight, own_start + low...  10.8 us
    dynamic_slice x4, local copies, waits for them, and re-layouts, features(): return lax.dynamic_slice_in_dim(rows, start, width, 1)  9.03 us
  transfers between devices with their start and end apart: 10, of which 5 were waited for; matrix products, arithmetic and copies ran while one was open for 25% of the time, Pallas kernels for 0%

profile of v1, /device:TPU:9, one launch (start us, length us, event | category | flops | bytes accessed | tf_op | source)
XLA Modules:
  0.0 268.0 jit_solution(604469756355748367)
XLA Ops:
  0.8 7.8 %fusion.1 = (f32[384]{0:T(512)S(1)}, bf16[384,8192]{1,0:T(8,128)(2,1)}) fusion(bf16[384,8192]{1,0:T(8,128)(2,1)} %param.6, f32[8192]{0:T(1024)S(1)} %convert_element_type.37), kind=kLoop, calls=%fused_computation.3 | loop fusion | flops 15728256 | bytes 12617216 | tf_op jit(solution)/shard_map/reduce_sum | solution.py:129
  13.7 14.5 %collective-permute-done.1 = bf16[384,1024]{1,0:T(8,128)(2,1)S(1)} collective-permute-done((bf16[384,1024]{1,0:T(8,128)(2,1)S(1)}, bf16[384,1024]{1,0:T(8,128)(2,1)S(1)}, u32[]{:S(2)}, u32[]{:S(2)}) %collective-permute-start.1) | collective-permute-done | bytes 786464 | tf_op jit(solution)/shard_map/ppermute | solution.py:52
  28.2 2.2 add_convert_fusion.1
  30.4 7.5 %all-to-all-start.1 = ((bf16[16,48,1024]{2,1,0:T(8,128)(2,1)}), bf16[16,48,1024]{2,1,0:T(8,128)(2,1)}, u32[]{:S(2)}, u32[]{:S(2)}) async-start(bf16[16,48,1024]{2,1,0:T(8,128)(2,1)} %bitcast.8), calls=%async_computation.1 | async-start | bytes 3145728 | tf_op jit(solution)/shard_map/all_to_all | solution.py:102
  37.9 3.0 %constant_dynamic-slice_fusion.1 = bf16[384,2560]{1,0:T(8,128)(2,1)} fusion(bf16[384,8192]{1,0:T(8,128)(2,1)} %get-tuple-element.8, s32[]{:T(128)S(6)} %select_n.113), kind=kLoop, calls=%fused_computation.69 | loop fusion | bytes 3932164 | tf_op jit(solution)/shard_map/dynamic_slice | solution.py:26
  42.1 3.7 %fusion.10 = f32[768,2560]{1,0:T(8,128)S(1)} fusion(bf16[384,8192]{1,0:T(8,128)(2,1)} %get-tuple-element.8, s32[]{:T(128)S(6)} %select_n.112, s32[384]{0:T(512)S(1)} %get-tuple-element.10), kind=kOutput, calls=%fused_computation.14 | convolution fusion | flops 1510244352 | bytes 9831940 | tf_op jit(solution)/shard_map/dot_general | solution.py:89
  45.8 39.3 %collective-permute-done.2 = bf16[384,2560]{1,0:T(8,128)(2,1)S(1)} collective-permute-done((bf16[384,2560]{1,0:T(8,128)(2,1)}, bf16[384,2560]{1,0:T(8,128)(2,1)S(1)}, u32[]{:S(2)}, u32[]{:S(2)}) %collective-permute-start.2) | collective-permute-done | bytes 1966112 | tf_op jit(solution)/shard_map/ppermute | solution.py:52
  85.1 4.2 %add_convert_fusion = bf16[768,2560]{1,0:T(8,128)(2,1)} fusion(f32[768,2560]{1,0:T(8,128)S(1)} %fusion.10, bf16[384,2560]{1,0:T(8,128)(2,1)S(1)} %collective-permute-done.2, s32[384]{0:T(512)S(1)} %get-tuple-element.9), kind=kOutput, calls=%fused_computation.6 | convolution fusion | flops 1514176512 | bytes 13764096 | tf_op jit(solution)/shard_map/dot_general | solution.py:95
  89.4 6.8 %all-to-all-start.2 = ((bf16[16,48,2560]{2,1,0:T(8,128)(2,1)}), bf16[16,48,2560]{2,1,0:T(8,128)(2,1)}, u32[]{:S(2)}, u32[]{:S(2)}) async-start(bf16[16,48,2560]{2,1,0:T(8,128)(2,1)} %bitcast.37), calls=%async_computation.2 | async-start | bytes 7864320 | tf_op jit(solution)/shard_map/all_to_all | solution.py:102
  98.5 3.8 %constant_dynamic-slice_fusion = bf16[384,4096]{1,0:T(8,128)(2,1)} fusion(bf16[384,8192]{1,0:T(8,128)(2,1)} %get-tuple-element.8, s32[]{:T(128)S(6)} %select_n.117), kind=kLoop, calls=%fused_computation.65 | loop fusion | bytes 6291460 | tf_op jit(solution)/shard_map/dynamic_slice | solution.py:26
  103.9 12.3 %fusion.51 = f32[384,1024]{1,0:T(8,128)S(1)} fusion(bf16[384,8192]{1,0:T(8,128)(2,1)} %get-tuple-element.8, bf16[8192,1024]{1,0:T(8,128)(2,1)} %param.8), kind=kOutput, calls=%fused_computation.89 | convolution fusion | flops 6442450944 | bytes 24641536 | tf_op jit(solution)/shard_map/dot_general | solution.py:126
  119.5 61.4 %all-to-all-done.2 = bf16[16,48,2560]{2,1,0:T(8,128)(2,1)} async-done(((bf16[16,48,2560]{2,1,0:T(8,128)(2,1)}), bf16[16,48,2560]{2,1,0:T(8,128)(2,1)}, u32[]{:S(2)}, u32[]{:S(2)}) %all-to-all-start.2) | async-done | bytes 3932192 | tf_op jit(solution)/shard_map/all_to_all | solution.py:102
  180.9 7.1 %all-to-all-start = ((bf16[16,48,512]{2,1,0:T(8,128)(2,1)}), bf16[16,48,512]{2,1,0:T(8,128)(2,1)S(1)}, u32[]{:S(2)}, u32[]{:S(2)}) async-start(bf16[16,48,512]{2,1,0:T(8,128)(2,1)} %bitcast.4), calls=%async_computation | async-start | bytes 1572864 | tf_op jit(solution)/shard_map/all_to_all | solution.py:102
  188.2 29.8 %all_gather.3 = s32[16,16,12]{2,1,0:T(8,128)S(1)} all-gather(s32[1,16,12]{2,1,0:T(8,128)S(1)} %sub.29), channel_id=1, replica_groups=mesh['adapter'=16,'tensor'=2] {'adapter'}, dimensions={0}, use_global_device_ids=true | all-gather | bytes 13056 | tf_op jit(solution)/shard_map/all_gather | solution.py:69
  218.4 4.0 %fusion.18 = f32[768,512]{0,1:T(8,128)} fusion(bf16[768,1024]{1,0:T(8,128)(2,1)} %bitcast.9, bf16[512,4096]{1,0:T(8,128)(2,1)} %bitcast.43), kind=kOutput, calls=%fused_computation.32 | convolution fusion | flops 805306368 | bytes 4194304 | tf_op jit(solution)/shard_map/dot_general | solution.py:103
  222.4 5.5 %fusion.6 = f32[768,512]{0,1:T(8,128)} fusion(bf16[768,2560]{1,0:T(8,128)(2,1)} %bitcast.12, bf16[512,4096]{1,0:T(8,128)(2,1)S(1)} %bitcast.45), kind=kOutput, calls=%fused_computation.10 | convolution fusion | flops 2013265920 | bytes 8126464 | tf_op jit(solution)/shard_map/dot_general | solution.py:103
  227.9 2.7 add_add_fusion.1
  232.0 2.9 %fusion.20 = f32[384,1024]{1,0:T(8,128)} fusion(bf16[384,512]{1,0:T(8,128)(2,1)S(1)} %collective-permute-done, bf16[8192,1024]{1,0:T(8,128)(2,1)} %param.8, s32[]{:T(128)S(6)} %select_n.105), kind=kOutput, calls=%fused_computation.34 | convolution fusion | flops 402653184 | bytes 3014660 | tf_op jit(solution)/shard_map/dot_general | solution.py:96
  234.9 2.2 collective-permute-done.3
  238.6 4.9 %all-to-all-start.3 = ((bf16[16,48,512]{2,1,0:T(8,128)(2,1)}), bf16[16,48,512]{2,1,0:T(8,128)(2,1)S(1)}, u32[]{:S(2)}, u32[]{:S(2)}) async-start(bf16[16,48,512]{2,1,0:T(8,128)(2,1)} %bitcast.42), calls=%async_computation.3 | async-start | bytes 1572864 | tf_op jit(solution)/shard_map/all_to_all | solution.py:147
  243.6 2.9 %fusion.8 = f32[384,1024]{1,0:T(8,128)S(1)} fusion(bf16[384,1024]{1,0:T(8,128)(2,1)} %copy-done.8, bf16[8192,1024]{1,0:T(8,128)(2,1)} %param.8, s32[]{:T(128)S(6)} %select_n.110), kind=kOutput, calls=%fused_computation.12 | convolution fusion | flops 805306368 | bytes 4456452 | tf_op jit(solution)/shard_map/dot_general | solution.py:96
  246.5 4.9 %fusion.4 = f32[384,1024]{1,0:T(8,128)S(1)} fusion(bf16[384,2560]{1,0:T(8,128)(2,1)S(1)} %copy-done.5, bf16[8192,1024]{1,0:T(8,128)(2,1)} %param.8, s32[]{:T(128)S(6)} %select_n.112), kind=kOutput, calls=%fused_computation.7 | convolution fusion | flops 2013265920 | bytes 8781828 | tf_op jit(solution)/shard_map/dot_general | solution.py:96
  251.5 6.8 %add_add_fusion = f32[384,1024]{1,0:T(8,128)S(1)} fusion(f32[384,1024]{1,0:T(8,128)S(1)} %fusion.4, f32[384,1024]{1,0:T(8,128)S(1)} %copy-done.6, f32[384,1024]{1,0:T(8,128)S(1)} %fusion.8, bf16[384,4096]{1,0:T(8,128)(2,1)} %collective-permute-done.4, bf16[8192,1024]{1,0:T(8,128)(2,1)} %param.8, s32[]{:T(128)S(6)} %select_n.109), kind=kOutput, calls=%fused_computation.22 | convolution fusion | flops 3222405120 | bytes 17825796 | tf_op jit(solution)/shard_map/dot_general | solution.py:121
  259.5 3.6 %all-to-all-done.3 = bf16[16,48,512]{2,1,0:T(8,128)(2,1)S(1)} async-done(((bf16[16,48,512]{2,1,0:T(8,128)(2,1)}), bf16[16,48,512]{2,1,0:T(8,128)(2,1)S(1)}, u32[]{:S(2)}, u32[]{:S(2)}) %all-to-all-start.3) | async-done | bytes 786464 | tf_op jit(solution)/shard_map/all_to_all | solution.py:147
  (68 shorter events, 23.6 us)
Async XLA Ops:
  0.0 237.1 %copy-start = (bf16[8,64,512]{2,1,0:T(8,128)(2,1)S(1)}, bf16[8,64,512]{2,1,0:T(8,128)(2,1)}, u32[]{:S(2)}) copy-start(bf16[8,64,512]{2,1,0:T(8,128)(2,1)} %param.10) | copy-start | bytes 1572868
  0.8 10.3 %copy-start.10 = (s32[192,1]{0,1:T(1,128)S(1)}, s32[192,1]{0,1:T(1,128)}, u32[]{:S(2)}) copy-start(s32[192,1]{0,1:T(1,128)} %param.11) | copy-start | bytes 2308
  9.8 18.5 %collective-permute-start.1 = (bf16[384,1024]{1,0:T(8,128)(2,1)S(1)}, bf16[384,1024]{1,0:T(8,128)(2,1)S(1)}, u32[]{:S(2)}, u32[]{:S(2)}) collective-permute-start(bf16[384,1024]{1,0:T(8,128)(2,1)S(1)} %constant_dynamic-slice_fusion.2), channel_id=1, source_target_pairs={{0,1},{1,0},{2,3},{3,2},{4,5},{5,4},{6,7},{7,6},{8,9},{9,8},{10,11... | collective-permute-start | bytes 2359304 | tf_op jit(solution)/shard_map/ppermute | solution.py:52
  28.2 2.2 copy-start.8
  30.4 59.0 %all-to-all-start.1 = ((bf16[16,48,1024]{2,1,0:T(8,128)(2,1)}), bf16[16,48,1024]{2,1,0:T(8,128)(2,1)}, u32[]{:S(2)}, u32[]{:S(2)}) async-start(bf16[16,48,1024]{2,1,0:T(8,128)(2,1)} %bitcast.8), calls=%async_computation.1 | async-start | bytes 3145728 | tf_op jit(solution)/shard_map/all_to_all | solution.py:102
  40.9 44.3 %collective-permute-start.2 = (bf16[384,2560]{1,0:T(8,128)(2,1)}, bf16[384,2560]{1,0:T(8,128)(2,1)S(1)}, u32[]{:S(2)}, u32[]{:S(2)}) collective-permute-start(bf16[384,2560]{1,0:T(8,128)(2,1)} %constant_dynamic-slice_fusion.1), channel_id=1, source_target_pairs={{0,1},{1,0},{2,3},{3,2},{4,5},{5,4},{6,7},{7,6},{8,9},{9,8},{10,11... | collective-permute-start | bytes 5898248 | tf_op jit(solution)/shard_map/ppermute | solution.py:52
  85.1 4.3 %copy-start.4 = (bf16[384,2560]{1,0:T(8,128)(2,1)}, bf16[384,2560]{1,0:T(8,128)(2,1)S(1)}, u32[]{:S(2)}) copy-start(bf16[384,2560]{1,0:T(8,128)(2,1)S(1)} %collective-permute-done.2) | copy-start | bytes 5898244
  89.4 91.5 %all-to-all-start.2 = ((bf16[16,48,2560]{2,1,0:T(8,128)(2,1)}), bf16[16,48,2560]{2,1,0:T(8,128)(2,1)}, u32[]{:S(2)}, u32[]{:S(2)}) async-start(bf16[16,48,2560]{2,1,0:T(8,128)(2,1)} %bitcast.37), calls=%async_computation.2 | async-start | bytes 7864320 | tf_op jit(solution)/shard_map/all_to_all | solution.py:102
  97.2 20.8 %collective-permute-start = (bf16[384,512]{1,0:T(8,128)(2,1)S(1)}, bf16[384,512]{1,0:T(8,128)(2,1)S(1)}, u32[]{:S(2)}, u32[]{:S(2)}) collective-permute-start(bf16[384,512]{1,0:T(8,128)(2,1)S(1)} %constant_dynamic-slice_fusion.3), channel_id=1, source_target_pairs={{0,1},{1,0},{2,3},{3,2},{4,5},{5,4},{6,7},{7,6},{8,9},{9,8},{10,11... | collective-permute-start | bytes 1179656 | tf_op jit(solution)/shard_map/ppermute | solution.py:52
  102.4 149.1 %collective-permute-start.4 = (bf16[384,4096]{1,0:T(8,128)(2,1)}, bf16[384,4096]{1,0:T(8,128)(2,1)}, u32[]{:S(2)}, u32[]{:S(2)}) collective-permute-start(bf16[384,4096]{1,0:T(8,128)(2,1)} %constant_dynamic-slice_fusion), channel_id=1, source_target_pairs={{0,1},{1,0},{2,3},{3,2},{4,5},{5,4},{6,7},{7,6},{8,9},{9,8},{10,11... | collective-permute-start | bytes 9437192 | tf_op jit(solution)/shard_map/ppermute | solution.py:52
  102.6 163.2 %collective-permute-start.5 = (f32[384]{0:T(512)S(1)}, f32[384]{0:T(512)S(1)}, u32[]{:S(2)}, u32[]{:S(2)}) collective-permute-start(f32[384]{0:T(512)S(1)} %add_rsqrt_fusion), channel_id=1, source_target_pairs={{0,1},{1,0},{2,3},{3,2},{4,5},{5,4},{6,7},{7,6},{8,9},{9,8},{10,11... | collective-permute-start | bytes 4616 | tf_op jit(solution)/shard_map/ppermute | solution.py:52
  116.1 147.0 %copy-start.1 = (f32[384,1024]{1,0:T(8,128)}, f32[384,1024]{1,0:T(8,128)S(1)}, u32[]{:S(2)}) copy-start(f32[384,1024]{1,0:T(8,128)S(1)} %fusion.51) | copy-start | bytes 4718596
  180.9 47.0 %all-to-all-start = ((bf16[16,48,512]{2,1,0:T(8,128)(2,1)}), bf16[16,48,512]{2,1,0:T(8,128)(2,1)S(1)}, u32[]{:S(2)}, u32[]{:S(2)}) async-start(bf16[16,48,512]{2,1,0:T(8,128)(2,1)} %bitcast.4), calls=%async_computation | async-start | bytes 1572864 | tf_op jit(solution)/shard_map/all_to_all | solution.py:102
  218.4 4.0 %copy-start.9 = (bf16[8,4096,64]{1,2,0:T(8,128)(2,1)S(1)}, bf16[8,4096,64]{1,2,0:T(8,128)(2,1)}, u32[]{:S(2)}) copy-start(bf16[8,4096,64]{1,2,0:T(8,128)(2,1)} %param.9) | copy-start | bytes 12582916
  230.7 6.4 %collective-permute-start.3 = (f32[64,768]{1,0:T(8,128)S(1)}, f32[64,768]{1,0:T(8,128)S(1)}, u32[]{:S(2)}, u32[]{:S(2)}) collective-permute-start(f32[64,768]{1,0:T(8,128)S(1)} %select_reduce_fusion), channel_id=1, source_target_pairs={{0,1},{1,0},{2,3},{3,2},{4,5},{5,4},{6,7},{7,6},{8,9},{9,8},{10,11... | collective-permute-start | bytes 589832 | tf_op jit(solution)/shard_map/ppermute | solution.py:52
  238.6 24.5 %all-to-all-start.3 = ((bf16[16,48,512]{2,1,0:T(8,128)(2,1)}), bf16[16,48,512]{2,1,0:T(8,128)(2,1)S(1)}, u32[]{:S(2)}, u32[]{:S(2)}) async-start(bf16[16,48,512]{2,1,0:T(8,128)(2,1)} %bitcast.42), calls=%async_computation.3 | async-start | bytes 1572864 | tf_op jit(solution)/shard_map/all_to_all | solution.py:147
  243.6 3.0 %copy-start.5 = (bf16[384,2560]{1,0:T(8,128)(2,1)S(1)}, bf16[384,2560]{1,0:T(8,128)(2,1)}, u32[]{:S(2)}) copy-start(bf16[384,2560]{1,0:T(8,128)(2,1)} %copy-done.4) | copy-start | bytes 5898244
  246.5 4.9 %copy-start.6 = (f32[384,1024]{1,0:T(8,128)S(1)}, f32[384,1024]{1,0:T(8,128)}, u32[]{:S(2)}) copy-start(f32[384,1024]{1,0:T(8,128)} %fusion.20) | copy-start | bytes 4718596
  258.3 1.2 copy-start.2
  263.1 1.4 copy-start.3
  264.5 1.1 slice-start
  265.1 1.9 slice-start.1
  265.8 1.1 copy-start.7

commit v2 on v1

--- a/solution.py
+++ b/solution.py
@@ -66,8 +66,9 @@
     hit = slot == request_slot[None, :]
     local = request_ids - holder * resident_adapters
     slot_local = jnp.sum(jnp.where(hit, local[None, :] + 1, 0), axis=1) - 1
-    told = lax.all_gather(slot_local.reshape(adapter_count, DEST), "adapter", axis=0)
-    told = lax.dynamic_index_in_dim(told, adapter_index, 1, keepdims=False)
+    told = lax.all_to_all(
+        slot_local.reshape(adapter_count, DEST), "adapter", split_axis=0, concat_axis=0, tiled=True
+    )
     slot_adapter = jnp.repeat(told.reshape(-1), DRAFT)
 
     def owner_slots(offset):
@@ -76,22 +77,29 @@
 
     place = [onehot(owner_slots(offset), slot_count) for offset in range(tensor_count)]
 
-    scaled = (
-        residual_rows.astype(jnp.float32) * norm_gain_vector.astype(jnp.float32)
-    ).astype(jnp.bfloat16)
+    def scaled(rows, start, width):
+        gain = lax.dynamic_slice_in_dim(norm_gain_vector, start, width, 0).astype(jnp.float32)
+        return (features(rows, start, width).astype(jnp.float32) * gain).astype(jnp.bfloat16)
 
     down = jnp.swapaxes(adapter_down_weight, 1, 2).reshape(resident_adapters * rank_width, share_width)
     partial_value = jnp.zeros((resident_adapters * rank_width, slot_count), jnp.float32)
     others = [jnp.zeros((own_tokens, 2 * column_block_width), jnp.float32) for _ in offsets]
     own_start = tensor_index * share_width
+    source = residual_rows
+    sent = told
     for low, high in chunk_bounds(share_width):
         width = high - low
+        pieces = [
+            to_offset(
+                scaled(source, (tensor_index + offset) % tensor_count * share_width + low, width), offset
+            )
+            for offset in offsets
+        ]
         outgoing = jnp.dot(
-            place[0], features(scaled, own_start + low, width), preferred_element_type=jnp.float32
+            place[0], scaled(source, own_start + low, width), preferred_element_type=jnp.float32
         )
-        for offset in offsets:
-            target = (tensor_index + offset) % tensor_count
-            piece = to_offset(features(scaled, target * share_width + low, width), offset)
+        source, *pieces = lax.optimization_barrier((source, *pieces))
+        for offset, piece in zip(offsets, pieces):
             outgoing += jnp.dot(place[offset], piece, preferred_element_type=jnp.float32)
             others[offset - 1] += jnp.dot(
                 piece,
@@ -99,10 +107,11 @@
                 preferred_element_type=jnp.float32,
             )
         outgoing = outgoing.astype(jnp.bfloat16).reshape(adapter_count, holder_slots, width)
-        received = lax.all_to_all(outgoing, "adapter", split_axis=0, concat_axis=0, tiled=True)
+        outgoing, sent = lax.optimization_barrier((outgoing, sent))
+        sent = lax.all_to_all(outgoing, "adapter", split_axis=0, concat_axis=0, tiled=True)
         partial_value += lax.dot_general(
             down[:, low:high],
-            received.reshape(slot_count, width),
+            sent.reshape(slot_count, width),
             (((1,), (1,)), ((), ())),
             preferred_element_type=jnp.float32,
         )
@@ -110,7 +119,7 @@
     for offset in offsets:
         target = (tensor_index + offset) % tensor_count
         rest = jnp.concatenate(
-            [features(scaled, (target + j) % tensor_count * share_width, share_width) for j in offsets],
+            [scaled(source, (target + j) % tensor_count * share_width, share_width) for j in offsets],
             axis=1,
         )
         rest = to_offset(rest, offset)
@@ -123,9 +132,11 @@
                 weight_rows,
                 preferred_element_type=jnp.float32,
             )
-    own = jnp.dot(scaled, key_value_weight, preferred_element_type=jnp.float32)
+    own = jnp.dot(
+        scaled(source, 0, model_width), key_value_weight, preferred_element_type=jnp.float32
+    )
 
-    values = residual_rows.astype(jnp.float32)
+    values = source.astype(jnp.float32)
     inverse = lax.rsqrt(jnp.mean(values * values, axis=-1) + EPS)
     inverse = [inverse] + [to_offset(inverse, offset) for offset in offsets]
 

time: 269 us -> 251 us (0.933)
  blocking collectives: 29.8 us -> 0 us
  starting transfers between devices: 32.8 us -> 43.5 us
  local copies, waits for them, and re-layouts: 13.4 us -> 5.52 us
  matrix products: 60.2 us -> 67.3 us
  other arithmetic: 10.4 us -> 14.1 us
    all_gather x1 -> x0, blocking collectives: 29.8 us -> none  [per_device(): lax.all_gather(slot_local.reshape(adapter_count, DEST), 'adapter', axis=0)]
    dynamic_slice x5 -> x0, local copies, waits for them, and re-layouts: 9.06 us -> none  [the longest x4 9.03 us: features(): return lax.dynamic_slice_in_dim(rows, start, width, 1)]
    convert_element_type x1 -> x9, other arithmetic: 0.78 us -> 8.35 us  [the longest x4 6.72 us: scaled(): (features(rows, start, width).astype(jnp.float32) * gain).astype(jnp.bflo...]
    all_to_all x0 -> x1, starting transfers between devices: none -> 6.85 us  [per_device(): lax.all_to_all(slot_local.reshape(adapter_count, DEST), 'adapter', split_...]
    reduce_sum x1, other arithmetic: 7.8 us -> 1.32 us  [per_device(): inverse = lax.rsqrt(jnp.mean(values * values, axis=-1) + EPS)]
    all_to_all x3, waiting for transfers between devices: 61.4 us -> 56.6 us  [per_device(): lax.all_to_all(outgoing, 'adapter', split_axis=0, concat_axis=0, tiled=True)]
    all_to_all x1, starting transfers between devices: 4.91 us -> 8.64 us  [per_device(): lax.all_to_all(correction.reshape(adapter_count, holder_slots, column_blo...]
    dot_general x3, matrix products: 7.88 us -> 11.6 us  [per_device(): jnp.dot(place[offset], piece, preferred_element_type=jnp.float32)]
  transfers between devices with their start and end apart: 10 -> 11, of which waited for: 5 -> 6; matrix products, arithmetic and copies ran while one was open for 25% -> 31% of each run, Pallas kernels for 0% -> 0%
where the time goes in v2:
time: 251 us
  waiting for transfers between devices  120 us (48%)
  matrix products  67.3 us (27%)
  starting transfers between devices  43.5 us (17%)
  other arithmetic  14.1 us (6%)
  local copies, waits for them, and re-layouts  5.52 us (2%)
    ppermute x6, waiting for transfers between devices, to_offset(): return lax.ppermute(value, 'tensor', pairs)  58.3 us
    all_to_all x3, waiting for transfers between devices, per_device(): lax.all_to_all(outgoing, 'adapter', split_axis=0, concat_axis=0, tiled=True)  56.6 us
    all_to_all x3, starting transfers between devices, per_device(): lax.all_to_all(outgoing, 'adapter', split_axis=0, concat_axis=0, tiled=True)  20.5 us
    dot_general x3, matrix products, per_device(): jnp.dot(piece, lax.dynamic_slice_in_dim(key_value_weight, own_start + low...  12.2 us
    dot_general x3, matrix products, per_device(): jnp.dot(place[offset], piece, preferred_element_type=jnp.float32)  11.6 us
    dot_general x1, matrix products, per_device(): jnp.dot(scaled(source, 0, model_width), key_value_weight, preferred_eleme...  11.4 us
    dot_general x3, matrix products, per_device(): lax.dot_general(down[:, low:high], sent.reshape(slot_count, width), (((1,...  11 us
    dot_general x3, matrix products, per_device(): jnp.dot(place[0], scaled(source, own_start + low, width), preferred_eleme...  10.6 us
  transfers between devices with their start and end apart: 11, of which 6 were waited for; matrix products, arithmetic and copies ran while one was open for 31% of the time, Pallas kernels for 0%

profile of v2, /device:TPU:9, one launch (start us, length us, event | category | flops | bytes accessed | tf_op | source)
XLA Modules:
  0.0 250.5 jit_solution(9388908633909492097)
XLA Ops:
  7.4 4.6 %collective-permute-done = bf16[384,512]{1,0:T(8,128)(2,1)S(1)} collective-permute-done((bf16[384,512]{1,0:T(8,128)(2,1)S(1)}, bf16[384,512]{1,0:T(8,128)(2,1)S(1)}, u32[]{:S(2)}, u32[]{:S(2)}) %collective-permute-start) | collective-permute-done | bytes 393248 | tf_op jit(solution)/shard_map/ppermute | solution.py:52
  13.4 7.5 %all-to-all-start.1 = ((bf16[16,48,512]{2,1,0:T(8,128)(2,1)}), bf16[16,48,512]{2,1,0:T(8,128)(2,1)S(1)}, u32[]{:S(2)}, u32[]{:S(2)}) async-start(bf16[16,48,512]{2,1,0:T(8,128)(2,1)} %bitcast.5), calls=%async_computation.1 | async-start | bytes 1572864 | tf_op jit(solution)/shard_map/all_to_all | solution.py:111
  23.6 2.1 fusion.21
  25.8 15.4 %collective-permute-done.1 = bf16[384,1024]{1,0:T(8,128)(2,1)S(1)} collective-permute-done((bf16[384,1024]{1,0:T(8,128)(2,1)S(1)}, bf16[384,1024]{1,0:T(8,128)(2,1)S(1)}, u32[]{:S(2)}, u32[]{:S(2)}) %collective-permute-start.1) | collective-permute-done | bytes 786464 | tf_op jit(solution)/shard_map/ppermute | solution.py:52
  42.1 2.1 add_convert_fusion.1
  44.3 6.8 %all-to-all-start.2 = ((bf16[16,48,1024]{2,1,0:T(8,128)(2,1)}), bf16[16,48,1024]{2,1,0:T(8,128)(2,1)}, u32[]{:S(2)}, u32[]{:S(2)}) async-start(bf16[16,48,1024]{2,1,0:T(8,128)(2,1)} %bitcast.9), calls=%async_computation.2 | async-start | bytes 3145728 | tf_op jit(solution)/shard_map/all_to_all | solution.py:111
  51.2 1.9 multiply_convert_fusion.2
  55.1 6.8 %fusion.13 = f32[768,2560]{1,0:T(8,128)} fusion(f32[2560]{0:T(1024)S(1)} %get-tuple-element.27, bf16[384,8192]{1,0:T(8,128)(2,1)} %param.6, s32[]{:T(128)S(6)} %select_n.115, s32[384]{0:T(512)S(1)} %get-tuple-element.30), kind=kOutput, calls=%fused_computation.19 | convolution fusion | flops 1513193472 | bytes 9842180 | tf_op jit(solution)/shard_map/dot_general | solution.py:98
  62.0 35.3 %collective-permute-done.2 = bf16[384,2560]{1,0:T(8,128)(2,1)} collective-permute-done((bf16[384,2560]{1,0:T(8,128)(2,1)S(1)}, bf16[384,2560]{1,0:T(8,128)(2,1)}, u32[]{:S(2)}, u32[]{:S(2)}) %collective-permute-start.2) | collective-permute-done | bytes 1966112 | tf_op jit(solution)/shard_map/ppermute | solution.py:52
  97.3 6.8 %all-to-all-start = ((s32[16,1,12]{2,1,0:T(1,128)}), s32[16,1,12]{2,1,0:T(1,128)S(1)}, u32[]{:S(2)}, u32[]{:S(2)}) async-start(s32[16,1,12]{2,1,0:T(1,128)} %bitcast.4), calls=%async_computation | async-start | bytes 16384 | tf_op jit(solution)/shard_map/all_to_all | solution.py:69
  104.1 8.0 %add_convert_fusion = bf16[768,2560]{1,0:T(8,128)(2,1)} fusion(f32[768,2560]{1,0:T(8,128)} %fusion.13, bf16[384,2560]{1,0:T(8,128)(2,1)} %collective-permute-done.2, s32[384]{0:T(512)S(1)} %get-tuple-element.29), kind=kOutput, calls=%fused_computation.6 | convolution fusion | flops 1514176512 | bytes 13764096 | tf_op jit(solution)/shard_map/dot_general | solution.py:103
  112.1 6.1 %all-to-all-start.3 = ((bf16[16,48,2560]{2,1,0:T(8,128)(2,1)}), bf16[16,48,2560]{2,1,0:T(8,128)(2,1)}, u32[]{:S(2)}, u32[]{:S(2)}) async-start(bf16[16,48,2560]{2,1,0:T(8,128)(2,1)} %bitcast.41), calls=%async_computation.3 | async-start | bytes 7864320 | tf_op jit(solution)/shard_map/all_to_all | solution.py:111
  120.3 3.2 %fusion.25 = f32[384,1024]{1,0:T(8,128)} fusion(bf16[384,512]{1,0:T(8,128)(2,1)} %copy-done.3, bf16[8192,1024]{1,0:T(8,128)(2,1)} %param.8, s32[]{:T(128)S(6)} %select_n.111), kind=kOutput, calls=%fused_computation.42 | convolution fusion | flops 402653184 | bytes 3014660 | tf_op jit(solution)/shard_map/dot_general | solution.py:104
  123.5 3.7 %fusion.11 = f32[384,1024]{1,0:T(8,128)} fusion(bf16[384,1024]{1,0:T(8,128)(2,1)S(1)} %copy-done.8, bf16[8192,1024]{1,0:T(8,128)(2,1)} %param.8, s32[]{:T(128)S(6)} %select_n.114), kind=kOutput, calls=%fused_computation.17 | convolution fusion | flops 805306368 | bytes 4456452 | tf_op jit(solution)/shard_map/dot_general | solution.py:104
  127.3 2.5 multiply_convert_fusion
  130.9 11.4 %fusion.4 = f32[384,1024]{1,0:T(8,128)} fusion(bf16[8192,1024]{1,0:T(8,128)(2,1)} %param.8, bf16[384,8192]{1,0:T(8,128)(2,1)S(1)} %bitcast.38, f32[8192]{0:T(1024)S(1)} %copy-done.10), kind=kOutput, calls=%fused_computation.7 | convolution fusion | flops 6451888128 | bytes 24674304 | tf_op jit(solution)/shard_map/dot_general | solution.py:135
  142.3 4.1 %fusion.23 = f32[768,512]{0,1:T(8,128)} fusion(bf16[768,1024]{1,0:T(8,128)(2,1)} %bitcast.10, bf16[512,4096]{1,0:T(8,128)(2,1)} %bitcast.46), kind=kOutput, calls=%fused_computation.40 | convolution fusion | flops 805306368 | bytes 4194304 | tf_op jit(solution)/shard_map/dot_general | solution.py:112
  146.4 56.6 %all-to-all-done.3 = bf16[16,48,2560]{2,1,0:T(8,128)(2,1)} async-done(((bf16[16,48,2560]{2,1,0:T(8,128)(2,1)}), bf16[16,48,2560]{2,1,0:T(8,128)(2,1)}, u32[]{:S(2)}, u32[]{:S(2)}) %all-to-all-start.3) | async-done | bytes 3932192 | tf_op jit(solution)/shard_map/all_to_all | solution.py:111
  202.9 5.3 %fusion.9 = f32[768,512]{0,1:T(8,128)S(1)} fusion(bf16[768,2560]{1,0:T(8,128)(2,1)} %bitcast.13, bf16[512,4096]{1,0:T(8,128)(2,1)} %bitcast.47), kind=kOutput, calls=%fused_computation.15 | convolution fusion | flops 2013265920 | bytes 8126464 | tf_op jit(solution)/shard_map/dot_general | solution.py:112
  212.7 3.0 %collective-permute-done.3 = f32[64,768]{1,0:T(8,128)S(1)} collective-permute-done((f32[64,768]{1,0:T(8,128)S(1)}, f32[64,768]{1,0:T(8,128)S(1)}, u32[]{:S(2)}, u32[]{:S(2)}) %collective-permute-start.3) | collective-permute-done | bytes 196640 | tf_op jit(solution)/shard_map/ppermute | solution.py:52
  217.2 8.6 %all-to-all-start.4 = ((bf16[16,48,512]{2,1,0:T(8,128)(2,1)}), bf16[16,48,512]{2,1,0:T(8,128)(2,1)S(1)}, u32[]{:S(2)}, u32[]{:S(2)}) async-start(bf16[16,48,512]{2,1,0:T(8,128)(2,1)} %bitcast.17), calls=%async_computation.4 | async-start | bytes 1572864 | tf_op jit(solution)/shard_map/all_to_all | solution.py:158
  227.1 5.3 %fusion.7 = f32[384,1024]{1,0:T(8,128)S(1)} fusion(bf16[384,2560]{1,0:T(8,128)(2,1)} %collective-permute-done.2, bf16[8192,1024]{1,0:T(8,128)(2,1)} %param.8, s32[]{:T(128)S(6)} %select_n.115), kind=kOutput, calls=%fused_computation.10 | convolution fusion | flops 2013265920 | bytes 8781828 | tf_op jit(solution)/shard_map/dot_general | solution.py:104
  232.4 6.9 %add_add_fusion = f32[384,1024]{1,0:T(8,128)S(1)} fusion(f32[384,1024]{1,0:T(8,128)S(1)} %fusion.7, f32[384,1024]{1,0:T(8,128)S(1)} %copy-done.4, f32[384,1024]{1,0:T(8,128)S(1)} %copy-done.11, bf16[384,4096]{1,0:T(8,128)(2,1)} %collective-permute-done.4, bf16[8192,1024]{1,0:T(8,128)(2,1)} %param.8, s32[]{:T(128)S(6)} %select_n.103), kind=kOutput, calls=%fused_computation.28 | convolution fusion | flops 3222405120 | bytes 17825796 | tf_op jit(solution)/shard_map/dot_general | solution.py:130
  240.5 4.9 %all-to-all-done.4 = bf16[16,48,512]{2,1,0:T(8,128)(2,1)S(1)} async-done(((bf16[16,48,512]{2,1,0:T(8,128)(2,1)}), bf16[16,48,512]{2,1,0:T(8,128)(2,1)S(1)}, u32[]{:S(2)}, u32[]{:S(2)}) %all-to-all-start.4) | async-done | bytes 786464 | tf_op jit(solution)/shard_map/all_to_all | solution.py:158
  (86 shorter events, 31.3 us)
Async XLA Ops:
  0.0 215.7 %copy-start = (bf16[8,64,512]{2,1,0:T(8,128)(2,1)S(1)}, bf16[8,64,512]{2,1,0:T(8,128)(2,1)}, u32[]{:S(2)}) copy-start(bf16[8,64,512]{2,1,0:T(8,128)(2,1)} %param.10) | copy-start | bytes 1572868
  1.9 10.0 %collective-permute-start = (bf16[384,512]{1,0:T(8,128)(2,1)S(1)}, bf16[384,512]{1,0:T(8,128)(2,1)S(1)}, u32[]{:S(2)}, u32[]{:S(2)}) collective-permute-start(bf16[384,512]{1,0:T(8,128)(2,1)S(1)} %multiply_convert_fusion.8), channel_id=1, source_target_pairs={{0,1},{1,0},{2,3},{3,2},{4,5},{5,4},{6,7},{7,6},{8,9},{9,8},{10,11... | collective-permute-start | bytes 1179656 | tf_op jit(solution)/shard_map/ppermute | solution.py:52
  12.0 9.0 %copy-start.9 = (bf16[8192]{0:T(1024)(128)(2,1)S(1)}, bf16[8192]{0:T(1024)(128)(2,1)}, u32[]{:S(2)}) copy-start(bf16[8192]{0:T(1024)(128)(2,1)} %param.7) | copy-start | bytes 49156
  13.4 30.8 %all-to-all-start.1 = ((bf16[16,48,512]{2,1,0:T(8,128)(2,1)}), bf16[16,48,512]{2,1,0:T(8,128)(2,1)S(1)}, u32[]{:S(2)}, u32[]{:S(2)}) async-start(bf16[16,48,512]{2,1,0:T(8,128)(2,1)} %bitcast.5), calls=%async_computation.1 | async-start | bytes 1572864 | tf_op jit(solution)/shard_map/all_to_all | solution.py:111
  22.4 18.8 %collective-permute-start.1 = (bf16[384,1024]{1,0:T(8,128)(2,1)S(1)}, bf16[384,1024]{1,0:T(8,128)(2,1)S(1)}, u32[]{:S(2)}, u32[]{:S(2)}) collective-permute-start(bf16[384,1024]{1,0:T(8,128)(2,1)S(1)} %multiply_convert_fusion.5), channel_id=1, source_target_pairs={{0,1},{1,0},{2,3},{3,2},{4,5},{5,4},{6,7},{7,6},{8,9},{9,8},{10,11... | collective-permute-start | bytes 2359304 | tf_op jit(solution)/shard_map/ppermute | solution.py:52
  44.3 53.0 %all-to-all-start.2 = ((bf16[16,48,1024]{2,1,0:T(8,128)(2,1)}), bf16[16,48,1024]{2,1,0:T(8,128)(2,1)}, u32[]{:S(2)}, u32[]{:S(2)}) async-start(bf16[16,48,1024]{2,1,0:T(8,128)(2,1)} %bitcast.9), calls=%async_computation.2 | async-start | bytes 3145728 | tf_op jit(solution)/shard_map/all_to_all | solution.py:111
  53.1 44.2 %collective-permute-start.2 = (bf16[384,2560]{1,0:T(8,128)(2,1)S(1)}, bf16[384,2560]{1,0:T(8,128)(2,1)}, u32[]{:S(2)}, u32[]{:S(2)}) collective-permute-start(bf16[384,2560]{1,0:T(8,128)(2,1)S(1)} %multiply_convert_fusion.2), channel_id=1, source_target_pairs={{0,1},{1,0},{2,3},{3,2},{4,5},{5,4},{6,7},{7,6},{8,9},{9,8},{10,11... | collective-permute-start | bytes 5898248 | tf_op jit(solution)/shard_map/ppermute | solution.py:52
  97.3 14.8 %all-to-all-start = ((s32[16,1,12]{2,1,0:T(1,128)}), s32[16,1,12]{2,1,0:T(1,128)S(1)}, u32[]{:S(2)}, u32[]{:S(2)}) async-start(s32[16,1,12]{2,1,0:T(1,128)} %bitcast.4), calls=%async_computation | async-start | bytes 16384 | tf_op jit(solution)/shard_map/all_to_all | solution.py:69
  112.1 15.2 %slice-start = ((s8[6291456]{0:T(1024)(128)(4,1)}), s8[2097152]{0:T(1024)(128)(4,1)S(1)}, s32[]{:S(2)}) async-start(s8[6291456]{0:T(1024)(128)(4,1)} %bitcast.37), calls=%async_computation.5 | async-start | bytes 4194304
  112.1 90.8 %all-to-all-start.3 = ((bf16[16,48,2560]{2,1,0:T(8,128)(2,1)}), bf16[16,48,2560]{2,1,0:T(8,128)(2,1)}, u32[]{:S(2)}, u32[]{:S(2)}) async-start(bf16[16,48,2560]{2,1,0:T(8,128)(2,1)} %bitcast.41), calls=%async_computation.3 | async-start | bytes 7864320 | tf_op jit(solution)/shard_map/all_to_all | solution.py:111
  120.2 3.3 %copy-start.8 = (bf16[384,1024]{1,0:T(8,128)(2,1)S(1)}, bf16[384,1024]{1,0:T(8,128)(2,1)}, u32[]{:S(2)}) copy-start(bf16[384,1024]{1,0:T(8,128)(2,1)} %copy-done.7) | copy-start | bytes 2359300
  120.3 7.0 %slice-start.1 = ((s8[6291456]{0:T(1024)(128)(4,1)}), s8[4194304]{0:T(1024)(128)(4,1)S(1)}, s32[]{:S(2)}) async-start(s8[6291456]{0:T(1024)(128)(4,1)} %bitcast.37), calls=%async_computation.6 | async-start | bytes 8388608
  127.3 3.7 %copy-start.10 = (f32[8192]{0:T(1024)S(1)}, f32[8192]{0:T(1024)}, u32[]{:S(2)}) copy-start(f32[8192]{0:T(1024)} %convert_element_type.109) | copy-start | bytes 98308
  129.7 102.7 %collective-permute-start.4 = (bf16[384,4096]{1,0:T(8,128)(2,1)}, bf16[384,4096]{1,0:T(8,128)(2,1)}, u32[]{:S(2)}, u32[]{:S(2)}) collective-permute-start(bf16[384,4096]{1,0:T(8,128)(2,1)} %multiply_convert_fusion), channel_id=1, source_target_pairs={{0,1},{1,0},{2,3},{3,2},{4,5},{5,4},{6,7},{7,6},{8,9},{9,8},{10,11... | collective-permute-start | bytes 9437192 | tf_op jit(solution)/shard_map/ppermute | solution.py:52
  142.3 69.0 %slice-start.2 = ((s8[6291456]{0:T(1024)(128)(4,1)}), s8[2097152]{0:T(1024)(128)(4,1)S(1)}, s32[]{:S(2)}) async-start(s8[6291456]{0:T(1024)(128)(4,1)} %bitcast.39), calls=%async_computation.7 | async-start | bytes 4194304
  202.9 5.3 %copy-start.6 = (f32[768,512]{0,1:T(8,128)S(1)}, f32[768,512]{0,1:T(8,128)}, u32[]{:S(2)}) copy-start(f32[768,512]{0,1:T(8,128)} %fusion.23) | copy-start | bytes 4718596
  202.9 8.4 %slice-start.3 = ((s8[6291456]{0:T(1024)(128)(4,1)}), s8[4194304]{0:T(1024)(128)(4,1)S(1)}, s32[]{:S(2)}) async-start(s8[6291456]{0:T(1024)(128)(4,1)} %bitcast.39), calls=%async_computation.8 | async-start | bytes 8388608
  210.1 5.6 %collective-permute-start.3 = (f32[64,768]{1,0:T(8,128)S(1)}, f32[64,768]{1,0:T(8,128)S(1)}, u32[]{:S(2)}, u32[]{:S(2)}) collective-permute-start(f32[64,768]{1,0:T(8,128)S(1)} %select_reduce_fusion), channel_id=1, source_target_pairs={{0,1},{1,0},{2,3},{3,2},{4,5},{5,4},{6,7},{7,6},{8,9},{9,8},{10,11... | collective-permute-start | bytes 589832 | tf_op jit(solution)/shard_map/ppermute | solution.py:52
  217.2 28.2 %all-to-all-start.4 = ((bf16[16,48,512]{2,1,0:T(8,128)(2,1)}), bf16[16,48,512]{2,1,0:T(8,128)(2,1)S(1)}, u32[]{:S(2)}, u32[]{:S(2)}) async-start(bf16[16,48,512]{2,1,0:T(8,128)(2,1)} %bitcast.17), calls=%async_computation.4 | async-start | bytes 1572864 | tf_op jit(solution)/shard_map/all_to_all | solution.py:158
  225.9 6.6 %copy-start.4 = (f32[384,1024]{1,0:T(8,128)S(1)}, f32[384,1024]{1,0:T(8,128)}, u32[]{:S(2)}) copy-start(f32[384,1024]{1,0:T(8,128)} %fusion.25) | copy-start | bytes 4718596
  225.9 6.6 %copy-start.11 = (f32[384,1024]{1,0:T(8,128)S(1)}, f32[384,1024]{1,0:T(8,128)}, u32[]{:S(2)}) copy-start(f32[384,1024]{1,0:T(8,128)} %fusion.11) | copy-start | bytes 4718596
  225.9 22.5 %collective-permute-start.5 = (f32[384]{0:T(512)S(1)}, f32[384]{0:T(512)S(1)}, u32[]{:S(2)}, u32[]{:S(2)}) collective-permute-start(f32[384]{0:T(512)S(1)} %add_rsqrt_fusion), channel_id=1, source_target_pairs={{0,1},{1,0},{2,3},{3,2},{4,5},{5,4},{6,7},{7,6},{8,9},{9,8},{10,11... | collective-permute-start | bytes 4616 | tf_op jit(solution)/shard_map/ppermute | solution.py:52
  240.5 6.5 %copy-start.1 = (f32[384,1024]{1,0:T(8,128)S(1)}, f32[384,1024]{1,0:T(8,128)}, u32[]{:S(2)}) copy-start(f32[384,1024]{1,0:T(8,128)} %fusion.4) | copy-start | bytes 4718596
  247.6 1.9 slice-start.5
  (5 other events, 5.9 us)

commit v3 on v2

--- a/solution.py
+++ b/solution.py
@@ -1,6 +1,10 @@
+import functools
+
 import jax
 import jax.numpy as jnp
 from jax import lax
+from jax.experimental import pallas as pl
+from jax.experimental.pallas import tpu as pltpu
 from jax.sharding import PartitionSpec as P
 
 DRAFT = 4
@@ -12,9 +16,13 @@
 
 
 def chunk_bounds(width):
-    first = max(width // 8, 128)
-    second = first + max(width // 4, 128)
+    first = max(width * 7 // 32 // 128, 1) * 128
+    second = first + max(width * 5 // 16 // 128, 1) * 128
     return [(0, first), (first, second), (second, width)]
+
+
+def after(value, *earlier):
+    return lax.optimization_barrier((value, *earlier))[0]
 
 
 def onehot(row_of_column, rows):
@@ -24,6 +32,75 @@
 
 def features(rows, start, width):
     return lax.dynamic_slice_in_dim(rows, start, width, 1)
+
+
+def shrink_kernel(adapters, down_ref, sent_ref, earlier_ref, slot_adapter_ref, out_ref):
+    rank_width, slots = out_ref.shape
+    step = 256 if slots % 256 == 0 else slots
+    for start in range(0, slots, step):
+        columns = slice(start, start + step)
+        partial_value = earlier_ref[:, columns] + lax.dot_general(
+            down_ref[...],
+            sent_ref[columns, :],
+            (((1,), (1,)), ((), ())),
+            preferred_element_type=jnp.float32,
+        )
+        named = slot_adapter_ref[:, columns]
+        chosen = jnp.zeros((rank_width, step), jnp.float32)
+        for adapter in range(adapters):
+            rows = partial_value[adapter * rank_width : (adapter + 1) * rank_width]
+            chosen = jnp.where(named == adapter, rows, chosen)
+        out_ref[:, columns] = chosen
+
+
+def shrink_last(down, sent, earlier, slot_adapter, adapters):
+    rows, width = down.shape
+    slots = sent.shape[0]
+    return pl.pallas_call(
+        functools.partial(shrink_kernel, adapters),
+        out_shape=jax.ShapeDtypeStruct((rows // adapters, slots), jnp.float32),
+        in_specs=[pl.BlockSpec(memory_space=pltpu.VMEM)] * 4,
+        out_specs=pl.BlockSpec(memory_space=pltpu.VMEM),
+        compiler_params=pltpu.CompilerParams(vmem_limit_bytes=16 * 1024 * 1024),
+        cost_estimate=pl.CostEstimate(
+            flops=2 * rows * width * slots,
+            bytes_accessed=(rows + slots) * width * 2 + rows * slots * 4,
+            transcendentals=0,
+        ),
+    )(down, sent, earlier, slot_adapter)
+
+
+def finish_kernel(count, owners_ref, *refs):
+    slots, factors, bases = refs[:count], refs[count : 2 * count], refs[2 * count : 3 * count]
+    returned_ref, out_ref = refs[3 * count :]
+    rows, width = bases[0].shape
+    half = width // 2
+    for i in range(count):
+        slot = lax.broadcasted_iota(jnp.int32, (rows, returned_ref.shape[0]), 1)
+        take = jnp.where(slot == slots[i][...], 1.0, 0.0).astype(jnp.bfloat16)
+        delta = jnp.dot(take, returned_ref[...], preferred_element_type=jnp.float32)
+        factor = factors[i][...]
+        place = pl.ds(pl.multiple_of(owners_ref[i] * rows, rows), rows)
+        out_ref[place, :half] = (bases[i][:, :half] * factor).astype(out_ref.dtype)
+        out_ref[place, half:] = ((bases[i][:, half:] + delta) * factor).astype(out_ref.dtype)
+
+
+def finish(owners, slots, factors, bases, returned):
+    count = len(bases)
+    rows, width = bases[0].shape
+    return pl.pallas_call(
+        functools.partial(finish_kernel, count),
+        out_shape=jax.ShapeDtypeStruct((rows * count, width), jnp.bfloat16),
+        in_specs=[pl.BlockSpec(memory_space=pltpu.SMEM)]
+        + [pl.BlockSpec(memory_space=pltpu.VMEM)] * (3 * count + 1),
+        out_specs=pl.BlockSpec(memory_space=pltpu.VMEM),
+        compiler_params=pltpu.CompilerParams(vmem_limit_bytes=16 * 1024 * 1024),
+        cost_estimate=pl.CostEstimate(
+            flops=2 * rows * count * returned.shape[0] * returned.shape[1],
+            bytes_accessed=rows * count * width * 6 + returned.size * 2,
+            transcendentals=0,
+        ),
+    )(owners, *slots, *factors, *bases, returned)
 
 
 def per_device(
@@ -82,23 +159,67 @@
         return (features(rows, start, width).astype(jnp.float32) * gain).astype(jnp.bfloat16)
 
     down = jnp.swapaxes(adapter_down_weight, 1, 2).reshape(resident_adapters * rank_width, share_width)
-    partial_value = jnp.zeros((resident_adapters * rank_width, slot_count), jnp.float32)
     others = [jnp.zeros((own_tokens, 2 * column_block_width), jnp.float32) for _ in offsets]
     own_start = tensor_index * share_width
-    source = residual_rows
-    sent = told
-    for low, high in chunk_bounds(share_width):
+    bounds = chunk_bounds(share_width)
+
+    def to_send(rows, low, width):
+        starts = [(tensor_index + offset) % tensor_count * share_width + low for offset in offsets]
+        return [scaled(rows, start, width) for start in starts]
+
+    def rest_of(offset):
+        target = (tensor_index + offset) % tensor_count
+        rest = [scaled(later_rows, (target + j) % tensor_count * share_width, share_width) for j in offsets]
+        starts = [(tensor_index + j) % tensor_count * share_width for j in offsets]
+        weight_rows = [
+            lax.dynamic_slice_in_dim(key_value_weight, start, share_width, 0) for start in starts
+        ]
+        return jnp.concatenate(rest, axis=1), jnp.concatenate(weight_rows, axis=0)
+
+    later_rows = after(residual_rows, slot_local)
+    parts = len(bounds)
+    rest_width = model_width - share_width
+    rest_cut = max(rest_width * 3 // 4 // 128, 1) * 128
+    rests = [rest_of(offset) for offset in offsets]
+    sending = [
+        to_send(residual_rows if part == 0 else later_rows, low, high - low)
+        for part, (low, high) in enumerate(bounds)
+    ]
+    sending.append([rest[:, :rest_cut] for rest, _ in rests])
+    own, inverse = None, []
+    partials = []
+    for part, (low, high) in enumerate(bounds):
         width = high - low
-        pieces = [
-            to_offset(
-                scaled(source, (tensor_index + offset) % tensor_count * share_width + low, width), offset
+        pieces = [to_offset(piece, offset) for offset, piece in zip(offsets, sending[part])]
+        outgoing = jnp.dot(
+            place[0],
+            scaled(residual_rows if part == 0 else later_rows, own_start + low, width),
+            preferred_element_type=jnp.float32,
+        ).astype(jnp.bfloat16)
+        if part == 0:
+            meanwhile = [told]
+        elif part == 1:
+            values = after(later_rows, *gate).astype(jnp.float32)
+            inverse = [lax.rsqrt(jnp.mean(values * values, axis=-1) + EPS)]
+            inverse += [to_offset(inverse[0], offset) for offset in offsets]
+            meanwhile = [*others, inverse[0]]
+        else:
+            own = jnp.dot(
+                scaled(after(later_rows, *gate), 0, model_width),
+                key_value_weight,
+                preferred_element_type=jnp.float32,
             )
-            for offset in offsets
-        ]
-        outgoing = jnp.dot(
-            place[0], scaled(source, own_start + low, width), preferred_element_type=jnp.float32
-        )
-        source, *pieces = lax.optimization_barrier((source, *pieces))
+            meanwhile = [*others, own, *inverse[1:]]
+        count = len(offsets)
+        tied = lax.optimization_barrier((*pieces, *sending[part + 1], outgoing, *meanwhile))
+        pieces, sending[part + 1] = tied[:count], tied[count : 2 * count]
+        gate = pieces
+        outgoing = tied[2 * count].astype(jnp.float32)
+        if part == 1:
+            others = list(tied[2 * count + 1 : 3 * count + 1])
+        elif part > 1:
+            others = list(tied[2 * count + 1 : 3 * count + 1])
+            own = tied[3 * count + 1]
         for offset, piece in zip(offsets, pieces):
             outgoing += jnp.dot(place[offset], piece, preferred_element_type=jnp.float32)
             others[offset - 1] += jnp.dot(
@@ -107,45 +228,37 @@
                 preferred_element_type=jnp.float32,
             )
         outgoing = outgoing.astype(jnp.bfloat16).reshape(adapter_count, holder_slots, width)
-        outgoing, sent = lax.optimization_barrier((outgoing, sent))
         sent = lax.all_to_all(outgoing, "adapter", split_axis=0, concat_axis=0, tiled=True)
-        partial_value += lax.dot_general(
-            down[:, low:high],
-            sent.reshape(slot_count, width),
-            (((1,), (1,)), ((), ())),
-            preferred_element_type=jnp.float32,
-        )
-
-    for offset in offsets:
-        target = (tensor_index + offset) % tensor_count
-        rest = jnp.concatenate(
-            [scaled(source, (target + j) % tensor_count * share_width, share_width) for j in offsets],
-            axis=1,
-        )
-        rest = to_offset(rest, offset)
-        for j in offsets:
-            weight_rows = lax.dynamic_slice_in_dim(
-                key_value_weight, (tensor_index + j) % tensor_count * share_width, share_width, 0
+        sent = sent.reshape(slot_count, width)
+        if part < parts - 1:
+            if partials:
+                sent = after(sent, partials[-1])
+            partial_value = lax.dot_general(
+                down[:, low:high], sent, (((1,), (1,)), ((), ())), preferred_element_type=jnp.float32
             )
-            others[offset - 1] += jnp.dot(
-                rest[:, (j - 1) * share_width : j * share_width],
-                weight_rows,
-                preferred_element_type=jnp.float32,
-            )
-    own = jnp.dot(
-        scaled(source, 0, model_width), key_value_weight, preferred_element_type=jnp.float32
-    )
-
-    values = source.astype(jnp.float32)
-    inverse = lax.rsqrt(jnp.mean(values * values, axis=-1) + EPS)
-    inverse = [inverse] + [to_offset(inverse, offset) for offset in offsets]
-
-    partial_value = partial_value.reshape(resident_adapters, rank_width, slot_count)
-    mine = jnp.arange(resident_adapters, dtype=jnp.int32)[:, None, None] == slot_adapter[None, None, :]
-    partial_value = jnp.sum(jnp.where(mine, partial_value, 0.0), axis=0)
+            partials.append(partial_value + partials[-1] if partials else partial_value)
+
+    early = [to_offset(piece, offset) for offset, piece in zip(offsets, sending[parts])]
+    low, high = bounds[-1]
+    sent, earlier_sum, last_down, *tied = lax.optimization_barrier(
+        (sent, partials[-1], down[:, low:high], *others, *early)
+    )
+    others, early = tied[: len(offsets)], tied[len(offsets) :]
+    partial_value = shrink_last(last_down, sent, earlier_sum, slot_adapter[None, :], resident_adapters)
     total = partial_value
     for offset in offsets:
         total += to_offset(partial_value, offset)
+
+    for offset in offsets:
+        rest, weight_rows = rests[offset - 1]
+        late = to_offset(after(rest[:, rest_cut:], total), offset)
+        for piece, piece_rows in (
+            (early[offset - 1], weight_rows[:rest_cut]),
+            (late, weight_rows[rest_cut:]),
+        ):
+            others[offset - 1] += jnp.dot(piece, piece_rows, preferred_element_type=jnp.float32)
+
+    mine = jnp.arange(resident_adapters, dtype=jnp.int32)[:, None, None] == slot_adapter[None, None, :]
     shrunk = total.astype(jnp.bfloat16)
     spread = jnp.where(mine, shrunk[None], jnp.zeros((), jnp.bfloat16))
     correction = lax.dot_general(
@@ -163,17 +276,14 @@
         tiled=True,
     ).reshape(slot_count, column_block_width)
 
-    result = jnp.zeros((own_tokens * tensor_count, 2 * column_block_width), jnp.bfloat16)
-    for offset, base in enumerate([own] + others):
-        delta = lax.dot_general(
-            place[offset], returned, (((0,), (0,)), ((), ())), preferred_element_type=jnp.float32
-        )
-        keys = base[:, :column_block_width]
-        vals = base[:, column_block_width:] + delta
-        rows = (jnp.concatenate([keys, vals], axis=1) * inverse[offset][:, None]).astype(jnp.bfloat16)
-        owner = (tensor_index - offset) % tensor_count
-        result = lax.dynamic_update_slice_in_dim(result, rows, owner * own_tokens, 0)
-    return result
+    owners = [(tensor_index - offset) % tensor_count for offset in range(tensor_count)]
+    return finish(
+        jnp.stack(owners).astype(jnp.int32),
+        [owner_slots(offset)[:, None] for offset in range(tensor_count)],
+        [column[:, None] for column in inverse],
+        [own] + others,
+        returned,
+    )
 
 
 def solution(mesh):

time: 251 us -> 244 us (0.972); the launches traced: 251 us -> 241 us
  waiting for transfers between devices: 120 us -> 103 us
  local copies, waits for them, and re-layouts: 5.52 us -> 20.6 us
  matrix products: 67.3 us -> 53 us
  Pallas kernels: 0 us -> 4.42 us
  other arithmetic: 14.1 us -> 18.2 us
    all_to_all x3, waiting for transfers between devices: 56.6 us -> 10.8 us  [per_device(): lax.all_to_all(outgoing, 'adapter', split_axis=0, concat_axis=0, tiled=True)]
    ppermute x6 -> x7, waiting for transfers between devices: 58.3 us -> 92.5 us  [to_offset(): return lax.ppermute(value, 'tensor', pairs)]
    dot_general x10 -> x8, matrix products: 42 us -> 32.3 us  [the longest x1 11.3 us: per_device(): jnp.dot(scaled(after(later_rows, *gate), 0, model_width), key_value_weigh...]
    unnamed x32 -> x40, local copies, waits for them, and re-layouts: 3.28 us -> 9.31 us
    slice x4 -> x3, local copies, waits for them, and re-layouts: 0.4 us -> 5.98 us  [the longest x1 2.95 us: per_device(): down[:, low:high]]
    all_to_all x1, waiting for transfers between devices: 4.85 us -> 0.01 us  [per_device(): lax.all_to_all(correction.reshape(adapter_count, holder_slots, column_blo...]
    pallas_call x0 -> x2, Pallas kernels: none -> 4.42 us  [the longest x1 2.6 us: finish(): pl.pallas_call(functools.partial(finish_kernel, count), out_shape=jax.Sha...]
    dot_general x3, matrix products: 11.6 us -> 7.94 us  [per_device(): jnp.dot(place[offset], piece, preferred_element_type=jnp.float32)]
  transfers between devices with their start and end apart: 11 -> 12, of which waited for: 6 -> 7; matrix products, arithmetic and copies ran while one was open for 31% -> 33% of each run, Pallas kernels for 0% -> 0%
where the time goes in v3:
time: 244 us; the launch traced here: 241 us
  waiting for transfers between devices  103 us (42%)
  matrix products  53 us (22%)
  starting transfers between devices  41.2 us (17%)
  local copies, waits for them, and re-layouts  20.6 us (8%)
  other arithmetic  18.2 us (7%)
  Pallas kernels  4.42 us (2%)
    ppermute x7, waiting for transfers between devices, to_offset(): return lax.ppermute(value, 'tensor', pairs)  92.5 us
    all_to_all x3, starting transfers between devices, per_device(): lax.all_to_all(outgoing, 'adapter', split_axis=0, concat_axis=0, tiled=True)  20.9 us
    dot_general x1, matrix products, per_device(): jnp.dot(scaled(after(later_rows, *gate), 0, model_width), key_value_weigh...  11.3 us
    dot_general x3, matrix products, per_device(): jnp.dot(piece, lax.dynamic_slice_in_dim(key_value_weight, own_start + low...  11.2 us
    all_to_all x3, waiting for transfers between devices, per_device(): lax.all_to_all(outgoing, 'adapter', split_axis=0, concat_axis=0, tiled=True)  10.8 us
    unnamed x40, local copies, waits for them, and re-layouts  9.31 us
    convert_element_type x4, other arithmetic, scaled(): (features(rows, start, width).astype(jnp.float32) * gain).astype(jnp.bflo...  9.17 us
    all_to_all x1, starting transfers between devices, per_device(): lax.all_to_all(correction.reshape(adapter_count, holder_slots, column_blo...  8.53 us
  transfers between devices with their start and end apart: 12, of which 7 were waited for; matrix products, arithmetic and copies ran while one was open for 33% of the time, Pallas kernels for 0%

profile of v3, /device:TPU:9, one launch (start us, length us, event | category | flops | bytes accessed | tf_op | source)
XLA Modules:
  0.0 241.0 jit_solution(1024184520788422704)
XLA Ops:
  2.5 6.6 %all-to-all-start.3 = ((s32[16,1,12]{2,1,0:T(1,128)}), s32[16,1,12]{2,1,0:T(1,128)S(1)}, u32[]{:S(2)}, u32[]{:S(2)}) async-start(s32[16,1,12]{2,1,0:T(1,128)} %bitcast.17), calls=%async_computation.3 | async-start | bytes 16384 | tf_op jit(solution)/shard_map/all_to_all | solution.py:146
  18.5 9.3 %collective-permute-done = bf16[384,896]{1,0:T(8,128)(2,1)S(1)} collective-permute-done((bf16[384,896]{1,0:T(8,128)(2,1)S(1)}, bf16[384,896]{1,0:T(8,128)(2,1)S(1)}, u32[]{:S(2)}, u32[]{:S(2)}) %collective-permute-start) | collective-permute-done | bytes 688160 | tf_op jit(solution)/shard_map/ppermute | solution.py:129
  29.8 7.0 %all-to-all-start.2 = ((bf16[16,48,896]{2,1,0:T(8,128)(2,1)}), bf16[16,48,896]{2,1,0:T(8,128)(2,1)}, u32[]{:S(2)}, u32[]{:S(2)}) async-start(bf16[16,48,896]{2,1,0:T(8,128)(2,1)} %bitcast.46), calls=%async_computation.2 | async-start | bytes 2752512 | tf_op jit(solution)/shard_map/all_to_all | solution.py:231
  39.5 2.8 %multiply_convert_fusion.4 = bf16[384,1920]{1,0:T(8,128)(2,1)} fusion(f32[1920]{0:T(1024)S(1)} %get-tuple-element.50, bf16[384,8192]{1,0:T(8,128)(2,1)} %param.6, s32[]{:T(128)S(6)} %select_n.112), kind=kLoop, calls=%fused_computation.14 | loop fusion | flops 2211840 | bytes 2956804 | tf_op jit(solution)/shard_map/convert_element_type | solution.py:159
  44.9 3.7 %fusion.10 = f32[384,1024]{1,0:T(8,128)} fusion(bf16[384,896]{1,0:T(8,128)(2,1)S(1)} %collective-permute-done, bf16[8192,1024]{1,0:T(8,128)(2,1)} %param.8, s32[]{:T(128)S(6)} %select_n.111), kind=kOutput, calls=%fused_computation.22 | convolution fusion | flops 704643072 | bytes 4096004 | tf_op jit(solution)/shard_map/dot_general | solution.py:225
  48.6 16.9 %collective-permute-done.2 = bf16[384,1280]{1,0:T(8,128)(2,1)S(1)} collective-permute-done((bf16[384,1280]{1,0:T(8,128)(2,1)S(1)}, bf16[384,1280]{1,0:T(8,128)(2,1)S(1)}, u32[]{:S(2)}, u32[]{:S(2)}) %collective-permute-start.2) | collective-permute-done | bytes 983072 | tf_op jit(solution)/shard_map/ppermute | solution.py:129
  68.9 6.9 %all-to-all-start.1 = ((bf16[16,48,1280]{2,1,0:T(8,128)(2,1)}), bf16[16,48,1280]{2,1,0:T(8,128)(2,1)}, u32[]{:S(2)}, u32[]{:S(2)}) async-start(bf16[16,48,1280]{2,1,0:T(8,128)(2,1)} %bitcast.45), calls=%async_computation.1 | async-start | bytes 3932160 | tf_op jit(solution)/shard_map/all_to_all | solution.py:231
  75.8 2.8 %multiply_convert_fusion.2 = bf16[384,4096]{1,0:T(8,128)(2,1)S(1)} fusion(f32[4096]{0:T(1024)S(1)} %dynamic-slice_convert_fusion, bf16[384,8192]{1,0:T(8,128)(2,1)} %param.6, s32[]{:T(128)S(6)} %select_n.115), kind=kLoop, calls=%fused_computation.6 | loop fusion | flops 4718592 | bytes 6307844 | tf_op jit(solution)/shard_map/convert_element_type | solution.py:159
  84.4 11.3 %fusion.refs_4_ = f32[384,1024]{1,0:T(8,128)} fusion(bf16[8192,1024]{1,0:T(8,128)(2,1)} %param.8, bf16[384,8192]{1,0:T(8,128)(2,1)S(1)} %bitcast.43, f32[8192]{0:T(1024)S(1)} %convert_element_type.140), kind=kOutput, calls=%fused_computation.2 | convolution fusion | flops 6451888128 | bytes 24674304 | tf_op jit(solution)/shard_map/dot_general | solution.py:207
  95.7 3.1 %fusion.6 = f32[384,1024]{1,0:T(8,128)S(1)} fusion(bf16[384,1280]{1,0:T(8,128)(2,1)S(1)} %copy-done.15, bf16[8192,1024]{1,0:T(8,128)(2,1)} %param.8, s32[]{:T(128)S(6)} %select_n.113), kind=kOutput, calls=%fused_computation.16 | convolution fusion | flops 1006632960 | bytes 5177348 | tf_op jit(solution)/shard_map/dot_general | solution.py:225
  100.2 17.2 %collective-permute-done.3 = bf16[384,1920]{1,0:T(8,128)(2,1)S(1)} collective-permute-done((bf16[384,1920]{1,0:T(8,128)(2,1)S(1)}, bf16[384,1920]{1,0:T(8,128)(2,1)S(1)}, u32[]{:S(2)}, u32[]{:S(2)}) %collective-permute-start.3) | collective-permute-done | bytes 1474592 | tf_op jit(solution)/shard_map/ppermute | solution.py:129
  118.5 3.4 %add_convert_fusion = bf16[768,1920]{1,0:T(8,128)(2,1)} fusion(bf16[768,1920]{1,0:T(8,128)(2,1)S(1)} %convolution_convert_fusion.1, bf16[384,1920]{1,0:T(8,128)(2,1)S(1)} %collective-permute-done.3, s32[384]{0:T(512)S(1)} %get-tuple-element.55), kind=kOutput, calls=%fused_computation.7 | convolution fusion | flops 1137180672 | bytes 7374336 | tf_op jit(solution)/shard_map/dot_general | solution.py:224
  121.9 7.1 %all-to-all-start = ((bf16[16,48,1920]{2,1,0:T(8,128)(2,1)}), bf16[16,48,1920]{2,1,0:T(8,128)(2,1)S(1)}, u32[]{:S(2)}, u32[]{:S(2)}) async-start(bf16[16,48,1920]{2,1,0:T(8,128)(2,1)} %bitcast.44), calls=%async_computation | async-start | bytes 5898240 | tf_op jit(solution)/shard_map/all_to_all | solution.py:231
  129.3 3.0 %slice.31.down_ref = bf16[512,1920]{1,0:T(8,128)(2,1)} slice(bf16[512,4096]{1,0:T(8,128)(2,1)} %bitcast.47), slice={[0:512], [2176:4096]} | slice | bytes 3932160 | tf_op jit(solution)/shard_map/slice | solution.py:244
  136.2 4.5 %fusion.4 = f32[384,1024]{1,0:T(8,128)S(1)} fusion(bf16[384,1920]{1,0:T(8,128)(2,1)} %copy-done.13, bf16[8192,1024]{1,0:T(8,128)(2,1)} %param.8, s32[]{:T(128)S(6)} %select_n.116), kind=kOutput, calls=%fused_computation.8 | convolution fusion | flops 1509949440 | bytes 6979588 | tf_op jit(solution)/shard_map/dot_general | solution.py:225
  145.8 3.9 %bitcast_add_fusion.earlier_ref = f32[512,768]{1,0:T(8,128)} fusion(f32[512,768]{1,0:T(8,128)S(1)} %convolution_bitcast_fusion, bf16[768,1280]{1,0:T(8,128)(2,1)} %bitcast.9, bf16[512,4096]{1,0:T(8,128)(2,1)S(1)} %bitcast.49), kind=kOutput, calls=%fused_computation.27 | convolution fusion | flops 1007026176 | bytes 6422528 | tf_op jit(solution)/shard_map/dot_general | solution.py:236
  149.8 32.1 %collective-permute-done.4 = bf16[384,3072]{1,0:T(8,128)(2,1)} collective-permute-done((bf16[384,3072]{1,0:T(8,128)(2,1)}, bf16[384,3072]{1,0:T(8,128)(2,1)}, u32[]{:S(2)}, u32[]{:S(2)}) %collective-permute-start.4) | collective-permute-done | bytes 2359328 | tf_op jit(solution)/shard_map/ppermute | solution.py:129
  181.8 10.8 %all-to-all-done = bf16[16,48,1920]{2,1,0:T(8,128)(2,1)S(1)} async-done(((bf16[16,48,1920]{2,1,0:T(8,128)(2,1)}), bf16[16,48,1920]{2,1,0:T(8,128)(2,1)S(1)}, u32[]{:S(2)}, u32[]{:S(2)}) %all-to-all-start) | async-done | bytes 2949152 | tf_op jit(solution)/shard_map/all_to_all | solution.py:231
  197.8 5.2 %collective-permute-done.5 = f32[64,768]{1,0:T(8,128)S(1)} collective-permute-done((f32[64,768]{1,0:T(8,128)S(1)}, f32[64,768]{1,0:T(8,128)S(1)}, u32[]{:S(2)}, u32[]{:S(2)}) %collective-permute-start.5) | collective-permute-done | bytes 196640 | tf_op jit(solution)/shard_map/ppermute | solution.py:129
  204.5 8.5 %all-to-all-start.4 = ((bf16[16,48,512]{2,1,0:T(8,128)(2,1)}), bf16[16,48,512]{2,1,0:T(8,128)(2,1)S(1)}, u32[]{:S(2)}, u32[]{:S(2)}) async-start(bf16[16,48,512]{2,1,0:T(8,128)(2,1)} %bitcast.19), calls=%async_computation.4 | async-start | bytes 1572864 | tf_op jit(solution)/shard_map/all_to_all | solution.py:271
  215.8 5.5 %fusion.1 = f32[384,1024]{1,0:T(8,128)S(1)} fusion(bf16[384,3072]{1,0:T(8,128)(2,1)} %collective-permute-done.4, bf16[8192,1024]{1,0:T(8,128)(2,1)} %param.8, s32[]{:T(128)S(6)} %select_n.109), kind=kOutput, calls=%fused_computation.3 | convolution fusion | flops 2415919104 | bytes 10223620 | tf_op jit(solution)/shard_map/dot_general | solution.py:259
  221.4 11.8 %collective-permute-done.6 = bf16[384,1024]{1,0:T(8,128)(2,1)} collective-permute-done((bf16[384,1024]{1,0:T(8,128)(2,1)S(1)}, bf16[384,1024]{1,0:T(8,128)(2,1)}, u32[]{:S(2)}, u32[]{:S(2)}) %collective-permute-start.6) | collective-permute-done | bytes 786464 | tf_op jit(solution)/shard_map/ppermute | solution.py:129
  233.2 2.8 %add_add_fusion.refs_5_ = f32[384,1024]{1,0:T(8,128)S(1)} fusion(f32[384,1024]{1,0:T(8,128)S(1)} %copy-done.7, f32[384,1024]{1,0:T(8,128)S(1)} %fusion.1, bf16[384,1024]{1,0:T(8,128)(2,1)} %collective-permute-done.6, bf16[8192,1024]{1,0:T(8,128)(2,1)} %param.8, s32[]{:T(128)S(6)} %add.237), kind=kOutput, calls=%fused_computation.28 | convolution fusion | flops 806092800 | bytes 7602180 | tf_op jit(solution)/shard_map/dot_general | solution.py:259
  238.4 2.6 %shard_map.65 = bf16[768,1024]{1,0:T(8,128)(2,1)} custom-call(s32[2]{0:T(128)S(1)} %pad_add_fusion.owners_ref, s32[384,1]{1,0:T(8,128)S(1)} %broadcast_in_dim.72.refs_0_, s32[384,1]{1,0:T(8,128)S(1)} %broadcast_in_dim.73.refs_1_, f32[384,1]{1,0:T(8,128)S(1)} %rsqrt.15.refs_2_, f32[384,1]{1,0:T(8,128)S(1)} %copy-done.4, f32[384,1024]{1,0:T(8,128)S(1)} %copy-done.2, ...), custom_call_target="tpu_custom_call" | custom-call | flops 603979776 | bytes 5505024 | tf_op jit(solution)/shard_map/pallas_call | solution.py:91
  (99 shorter events, 51.9 us)
Async XLA Ops:
  0.0 203.0 %copy-start = (bf16[8,64,512]{2,1,0:T(8,128)(2,1)S(1)}, bf16[8,64,512]{2,1,0:T(8,128)(2,1)}, u32[]{:S(2)}) copy-start(bf16[8,64,512]{2,1,0:T(8,128)(2,1)} %param.10) | copy-start | bytes 1572868
  2.5 27.4 %all-to-all-start.3 = ((s32[16,1,12]{2,1,0:T(1,128)}), s32[16,1,12]{2,1,0:T(1,128)S(1)}, u32[]{:S(2)}, u32[]{:S(2)}) async-start(s32[16,1,12]{2,1,0:T(1,128)} %bitcast.17), calls=%async_computation.3 | async-start | bytes 16384 | tf_op jit(solution)/shard_map/all_to_all | solution.py:146
  11.1 16.7 %collective-permute-start = (bf16[384,896]{1,0:T(8,128)(2,1)S(1)}, bf16[384,896]{1,0:T(8,128)(2,1)S(1)}, u32[]{:S(2)}, u32[]{:S(2)}) collective-permute-start(bf16[384,896]{1,0:T(8,128)(2,1)S(1)} %multiply_convert_fusion.9), channel_id=1, source_target_pairs={{0,1},{1,0},{2,3},{3,2},{4,5},{5,4},{6,7},{7,6},{8,9},{9,8},{10,11... | collective-permute-start | bytes 2064392 | tf_op jit(solution)/shard_map/ppermute | solution.py:129
  29.8 7.0 %copy-start.12 = (bf16[8192]{0:T(1024)(128)(2,1)S(1)}, bf16[8192]{0:T(1024)(128)(2,1)}, u32[]{:S(2)}) copy-start(bf16[8192]{0:T(1024)(128)(2,1)} %param.7) | copy-start | bytes 49156
  29.8 13.7 %slice-start = ((s8[6291456]{0:T(1024)(128)(4,1)}), s8[2097152]{0:T(1024)(128)(4,1)S(1)}, s32[]{:S(2)}) async-start(s8[6291456]{0:T(1024)(128)(4,1)} %bitcast.40), calls=%async_computation.5 | async-start | bytes 4194304
  29.8 39.1 %all-to-all-start.2 = ((bf16[16,48,896]{2,1,0:T(8,128)(2,1)}), bf16[16,48,896]{2,1,0:T(8,128)(2,1)}, u32[]{:S(2)}, u32[]{:S(2)}) async-start(bf16[16,48,896]{2,1,0:T(8,128)(2,1)} %bitcast.46), calls=%async_computation.2 | async-start | bytes 2752512 | tf_op jit(solution)/shard_map/all_to_all | solution.py:231
  37.0 6.6 %slice-start.1 = ((s8[6291456]{0:T(1024)(128)(4,1)}), s8[4194304]{0:T(1024)(128)(4,1)S(1)}, s32[]{:S(2)}) async-start(s8[6291456]{0:T(1024)(128)(4,1)} %bitcast.40), calls=%async_computation.6 | async-start | bytes 8388608
  39.5 2.8 %copy-start.10 = (bf16[384,1280]{1,0:T(8,128)(2,1)S(1)}, bf16[384,1280]{1,0:T(8,128)(2,1)}, u32[]{:S(2)}) copy-start(bf16[384,1280]{1,0:T(8,128)(2,1)} %multiply_convert_fusion.6) | copy-start | bytes 2949124
  42.4 23.1 %collective-permute-start.2 = (bf16[384,1280]{1,0:T(8,128)(2,1)S(1)}, bf16[384,1280]{1,0:T(8,128)(2,1)S(1)}, u32[]{:S(2)}, u32[]{:S(2)}) collective-permute-start(bf16[384,1280]{1,0:T(8,128)(2,1)S(1)} %copy-done.10), channel_id=1, source_target_pairs={{0,1},{1,0},{2,3},{3,2},{4,5},{5,4},{6,7},{7,6},{8,9},{9,8},{10,11... | collective-permute-start | bytes 2949128 | tf_op jit(solution)/shard_map/ppermute | solution.py:129
  68.9 12.1 %slice-start.2 = ((s8[6291456]{0:T(1024)(128)(4,1)}), s8[2097152]{0:T(1024)(128)(4,1)S(1)}, s32[]{:S(2)}) async-start(s8[6291456]{0:T(1024)(128)(4,1)} %bitcast.42), calls=%async_computation.7 | async-start | bytes 4194304
  68.9 53.0 %all-to-all-start.1 = ((bf16[16,48,1280]{2,1,0:T(8,128)(2,1)}), bf16[16,48,1280]{2,1,0:T(8,128)(2,1)}, u32[]{:S(2)}, u32[]{:S(2)}) async-start(bf16[16,48,1280]{2,1,0:T(8,128)(2,1)} %bitcast.45), calls=%async_computation.1 | async-start | bytes 3932160 | tf_op jit(solution)/shard_map/all_to_all | solution.py:231
  75.8 5.2 %slice-start.3 = ((s8[6291456]{0:T(1024)(128)(4,1)}), s8[4194304]{0:T(1024)(128)(4,1)S(1)}, s32[]{:S(2)}) async-start(s8[6291456]{0:T(1024)(128)(4,1)} %bitcast.42), calls=%async_computation.8 | async-start | bytes 8388608
  81.0 3.0 %copy-start.9 = (bf16[384,1920]{1,0:T(8,128)(2,1)S(1)}, bf16[384,1920]{1,0:T(8,128)(2,1)}, u32[]{:S(2)}) copy-start(bf16[384,1920]{1,0:T(8,128)(2,1)} %multiply_convert_fusion.4) | copy-start | bytes 4423684
  82.8 12.9 %copy-start.15 = (bf16[384,1280]{1,0:T(8,128)(2,1)S(1)}, bf16[384,1280]{1,0:T(8,128)(2,1)}, u32[]{:S(2)}) copy-start(bf16[384,1280]{1,0:T(8,128)(2,1)} %copy-done.14) | copy-start | bytes 2949124
  82.8 17.4 %collective-permute-start.1 = (f32[384]{0:T(512)S(1)}, f32[384]{0:T(512)S(1)}, u32[]{:S(2)}, u32[]{:S(2)}) collective-permute-start(f32[384]{0:T(512)S(1)} %add_rsqrt_fusion), channel_id=1, source_target_pairs={{0,1},{1,0},{2,3},{3,2},{4,5},{5,4},{6,7},{7,6},{8,9},{9,8},{10,11... | collective-permute-start | bytes 4616 | tf_op jit(solution)/shard_map/ppermute | solution.py:129
  84.1 33.3 %collective-permute-start.3 = (bf16[384,1920]{1,0:T(8,128)(2,1)S(1)}, bf16[384,1920]{1,0:T(8,128)(2,1)S(1)}, u32[]{:S(2)}, u32[]{:S(2)}) collective-permute-start(bf16[384,1920]{1,0:T(8,128)(2,1)S(1)} %copy-done.9), channel_id=1, source_target_pairs={{0,1},{1,0},{2,3},{3,2},{4,5},{5,4},{6,7},{7,6},{8,9},{9,8},{10,11... | collective-permute-start | bytes 4423688 | tf_op jit(solution)/shard_map/ppermute | solution.py:129
  95.7 3.1 %copy-start.8 = (f32[384,1024]{1,0:T(8,128)S(1)}, f32[384,1024]{1,0:T(8,128)}, u32[]{:S(2)}) copy-start(f32[384,1024]{1,0:T(8,128)} %fusion.10) | copy-start | bytes 4718596
  121.9 70.7 %all-to-all-start = ((bf16[16,48,1920]{2,1,0:T(8,128)(2,1)}), bf16[16,48,1920]{2,1,0:T(8,128)(2,1)S(1)}, u32[]{:S(2)}, u32[]{:S(2)}) async-start(bf16[16,48,1920]{2,1,0:T(8,128)(2,1)} %bitcast.44), calls=%async_computation | async-start | bytes 5898240 | tf_op jit(solution)/shard_map/all_to_all | solution.py:231
  129.0 52.8 %collective-permute-start.4 = (bf16[384,3072]{1,0:T(8,128)(2,1)}, bf16[384,3072]{1,0:T(8,128)(2,1)}, u32[]{:S(2)}, u32[]{:S(2)}) collective-permute-start(bf16[384,3072]{1,0:T(8,128)(2,1)} %slice.28), channel_id=1, source_target_pairs={{0,1},{1,0},{2,3},{3,2},{4,5},{5,4},{6,7},{7,6},{8,9},{9,8},{10,11... | collective-permute-start | bytes 7077896 | tf_op jit(solution)/shard_map/ppermute | solution.py:129
  136.2 4.5 %copy-start.6 = (f32[384,1024]{1,0:T(8,128)S(1)}, f32[384,1024]{1,0:T(8,128)}, u32[]{:S(2)}) copy-start(f32[384,1024]{1,0:T(8,128)} %add.223) | copy-start | bytes 4718596
  197.4 5.6 %collective-permute-start.5 = (f32[64,768]{1,0:T(8,128)S(1)}, f32[64,768]{1,0:T(8,128)S(1)}, u32[]{:S(2)}, u32[]{:S(2)}) collective-permute-start(f32[64,768]{1,0:T(8,128)S(1)} %shard_map.64), channel_id=1, source_target_pairs={{0,1},{1,0},{2,3},{3,2},{4,5},{5,4},{6,7},{7,6},{8,9},{9,8},{10,11... | collective-permute-start | bytes 589832 | tf_op jit(solution)/shard_map/ppermute | solution.py:129
  204.5 31.5 %all-to-all-start.4 = ((bf16[16,48,512]{2,1,0:T(8,128)(2,1)}), bf16[16,48,512]{2,1,0:T(8,128)(2,1)S(1)}, u32[]{:S(2)}, u32[]{:S(2)}) async-start(bf16[16,48,512]{2,1,0:T(8,128)(2,1)} %bitcast.19), calls=%async_computation.4 | async-start | bytes 1572864 | tf_op jit(solution)/shard_map/all_to_all | solution.py:271
  214.3 18.9 %collective-permute-start.6 = (bf16[384,1024]{1,0:T(8,128)(2,1)S(1)}, bf16[384,1024]{1,0:T(8,128)(2,1)}, u32[]{:S(2)}, u32[]{:S(2)}) collective-permute-start(bf16[384,1024]{1,0:T(8,128)(2,1)S(1)} %slice.32), channel_id=1, source_target_pairs={{0,1},{1,0},{2,3},{3,2},{4,5},{5,4},{6,7},{7,6},{8,9},{9,8},{10,11... | collective-permute-start | bytes 2359304 | tf_op jit(solution)/shard_map/ppermute | solution.py:129
  215.8 17.4 %copy-start.7 = (f32[384,1024]{1,0:T(8,128)S(1)}, f32[384,1024]{1,0:T(8,128)}, u32[]{:S(2)}) copy-start(f32[384,1024]{1,0:T(8,128)} %add.228) | copy-start | bytes 4718596
  (8 other events, 12.5 us)

commit v4 on v3

--- a/solution.py
+++ b/solution.py
@@ -167,59 +167,53 @@
         starts = [(tensor_index + offset) % tensor_count * share_width + low for offset in offsets]
         return [scaled(rows, start, width) for start in starts]
 
-    def rest_of(offset):
+    def rest_of(offset, rows):
         target = (tensor_index + offset) % tensor_count
-        rest = [scaled(later_rows, (target + j) % tensor_count * share_width, share_width) for j in offsets]
+        rest = [scaled(rows, (target + j) % tensor_count * share_width, share_width) for j in offsets]
+        return jnp.concatenate(rest, axis=1)
+
+    def rest_weight():
         starts = [(tensor_index + j) % tensor_count * share_width for j in offsets]
-        weight_rows = [
-            lax.dynamic_slice_in_dim(key_value_weight, start, share_width, 0) for start in starts
-        ]
-        return jnp.concatenate(rest, axis=1), jnp.concatenate(weight_rows, axis=0)
+        return jnp.concatenate(
+            [lax.dynamic_slice_in_dim(key_value_weight, start, share_width, 0) for start in starts], axis=0
+        )
+
+    def own_product(rows, low, high):
+        return jnp.dot(
+            scaled(rows, low, high - low), key_value_weight[low:high], preferred_element_type=jnp.float32
+        )
 
     later_rows = after(residual_rows, slot_local)
     parts = len(bounds)
     rest_width = model_width - share_width
-    rest_cut = max(rest_width * 3 // 4 // 128, 1) * 128
-    rests = [rest_of(offset) for offset in offsets]
+    rest_cut = max(rest_width * 13 // 16 // 128, 1) * 128
     sending = [
         to_send(residual_rows if part == 0 else later_rows, low, high - low)
         for part, (low, high) in enumerate(bounds)
     ]
-    sending.append([rest[:, :rest_cut] for rest, _ in rests])
-    own, inverse = None, []
+    own, inverse, gate = None, [], ()
     partials = []
     for part, (low, high) in enumerate(bounds):
         width = high - low
+        sending[part] = [after(piece, *gate) for piece in sending[part]]
         pieces = [to_offset(piece, offset) for offset, piece in zip(offsets, sending[part])]
         outgoing = jnp.dot(
             place[0],
             scaled(residual_rows if part == 0 else later_rows, own_start + low, width),
             preferred_element_type=jnp.float32,
         ).astype(jnp.bfloat16)
+        outgoing = lax.optimization_barrier(outgoing).astype(jnp.float32)
         if part == 0:
-            meanwhile = [told]
+            pieces = [after(piece, told) for piece in pieces]
         elif part == 1:
             values = after(later_rows, *gate).astype(jnp.float32)
             inverse = [lax.rsqrt(jnp.mean(values * values, axis=-1) + EPS)]
             inverse += [to_offset(inverse[0], offset) for offset in offsets]
-            meanwhile = [*others, inverse[0]]
+            pieces = [after(piece, inverse[0]) for piece in pieces]
         else:
-            own = jnp.dot(
-                scaled(after(later_rows, *gate), 0, model_width),
-                key_value_weight,
-                preferred_element_type=jnp.float32,
-            )
-            meanwhile = [*others, own, *inverse[1:]]
-        count = len(offsets)
-        tied = lax.optimization_barrier((*pieces, *sending[part + 1], outgoing, *meanwhile))
-        pieces, sending[part + 1] = tied[:count], tied[count : 2 * count]
+            own = own_product(after(later_rows, *gate), 0, model_width // 2)
+            own, *pieces = lax.optimization_barrier((own, *pieces))
         gate = pieces
-        outgoing = tied[2 * count].astype(jnp.float32)
-        if part == 1:
-            others = list(tied[2 * count + 1 : 3 * count + 1])
-        elif part > 1:
-            others = list(tied[2 * count + 1 : 3 * count + 1])
-            own = tied[3 * count + 1]
         for offset, piece in zip(offsets, pieces):
             outgoing += jnp.dot(place[offset], piece, preferred_element_type=jnp.float32)
             others[offset - 1] += jnp.dot(
@@ -238,20 +232,26 @@
             )
             partials.append(partial_value + partials[-1] if partials else partial_value)
 
-    early = [to_offset(piece, offset) for offset, piece in zip(offsets, sending[parts])]
+    early = [
+        to_offset(after(rest_of(offset, later_rows)[:, :rest_cut], *gate), offset) for offset in offsets
+    ]
     low, high = bounds[-1]
     sent, earlier_sum, last_down, *tied = lax.optimization_barrier(
-        (sent, partials[-1], down[:, low:high], *others, *early)
-    )
-    others, early = tied[: len(offsets)], tied[len(offsets) :]
+        (sent, partials[-1], down[:, low:high], *others, *inverse[1:], *early)
+    )
+    count = len(offsets)
+    others, inverse[1:], early = tied[:count], tied[count : 2 * count], tied[2 * count :]
     partial_value = shrink_last(last_down, sent, earlier_sum, slot_adapter[None, :], resident_adapters)
     total = partial_value
     for offset in offsets:
         total += to_offset(partial_value, offset)
 
+    weight_rows = rest_weight()
+    last_rows = after(later_rows, total)
+    own += own_product(last_rows, model_width // 2, model_width)
     for offset in offsets:
-        rest, weight_rows = rests[offset - 1]
-        late = to_offset(after(rest[:, rest_cut:], total), offset)
+        late = to_offset(rest_of(offset, last_rows)[:, rest_cut:], offset)
+        late, own = lax.optimization_barrier((late, own))
         for piece, piece_rows in (
             (early[offset - 1], weight_rows[:rest_cut]),
             (late, weight_rows[rest_cut:]),

time: 244 us -> 230 us (0.943)
  waiting for transfers between devices: 103 us -> 85.1 us
  matrix products: 53 us -> 62.2 us
    ppermute x7, waiting for transfers between devices: 92.5 us -> 75.5 us  [to_offset(): return lax.ppermute(value, 'tensor', pairs)]
    dot_general x1 -> x2, matrix products: 11.3 us -> 15.9 us  [own_product(): jnp.dot(scaled(rows, low, high - low), key_value_weight[low:high], prefer...]
    slice x2 -> x1, local copies, waits for them, and re-layouts: 3.03 us -> 0.01 us  [per_device(): late = to_offset(rest_of(offset, last_rows)[:, rest_cut:], offset)]
    dot_general x3, matrix products: 6.33 us -> 9.13 us  [per_device(): jnp.dot(place[0], scaled(residual_rows if part == 0 else later_rows, own_...]
    all_to_all x3, waiting for transfers between devices: 10.8 us -> 8.1 us  [per_device(): lax.all_to_all(outgoing, 'adapter', split_axis=0, concat_axis=0, tiled=True)]
    convert_element_type x4 -> x5, other arithmetic: 9.17 us -> 10.3 us  [scaled(): (features(rows, start, width).astype(jnp.float32) * gain).astype(jnp.bflo...]
    unnamed x40 -> x42, local copies, waits for them, and re-layouts: 9.31 us -> 8.55 us
  transfers between devices with their start and end apart: 12 -> 12, of which waited for: 7 -> 9; matrix products, arithmetic and copies ran while one was open for 33% -> 38% of each run, Pallas kernels for 0% -> 0%
where the time goes in v4:
time: 230 us; the launch traced here: 228 us
  waiting for transfers between devices  85.1 us (37%)
  matrix products  62.2 us (27%)
  starting transfers between devices  40.2 us (17%)
  local copies, waits for them, and re-layouts  18.9 us (8%)
  other arithmetic  17.2 us (7%)
  Pallas kernels  4.47 us (2%)
    ppermute x7, waiting for transfers between devices, to_offset(): return lax.ppermute(value, 'tensor', pairs)  75.5 us
    all_to_all x3, starting transfers between devices, per_device(): lax.all_to_all(outgoing, 'adapter', split_axis=0, concat_axis=0, tiled=True)  19.1 us
    dot_general x2, matrix products, own_product(): jnp.dot(scaled(rows, low, high - low), key_value_weight[low:high], prefer...  15.9 us
    dot_general x3, matrix products, per_device(): jnp.dot(piece, lax.dynamic_slice_in_dim(key_value_weight, own_start + low...  11.4 us
    convert_element_type x5, other arithmetic, scaled(): (features(rows, start, width).astype(jnp.float32) * gain).astype(jnp.bflo...  10.3 us
    dot_general x2, matrix products, per_device(): jnp.dot(piece, piece_rows, preferred_element_type=jnp.float32)  9.93 us
    dot_general x3, matrix products, per_device(): jnp.dot(place[offset], piece, preferred_element_type=jnp.float32)  9.3 us
    dot_general x3, matrix products, per_device(): jnp.dot(place[0], scaled(residual_rows if part == 0 else later_rows, own_...  9.13 us
  transfers between devices with their start and end apart: 12, of which 9 were waited for; matrix products, arithmetic and copies ran while one was open for 38% of the time, Pallas kernels for 0%

profile of v4, /device:TPU:9, one launch (start us, length us, event | category | flops | bytes accessed | tf_op | source)
XLA Modules:
  0.0 228.2 jit_solution(7765866229883719184)
XLA Ops:
  5.7 6.9 %all-to-all-start.3 = ((s32[16,1,12]{2,1,0:T(1,128)}), s32[16,1,12]{2,1,0:T(1,128)S(1)}, u32[]{:S(2)}, u32[]{:S(2)}) async-start(s32[16,1,12]{2,1,0:T(1,128)} %bitcast.17), calls=%async_computation.3 | async-start | bytes 16384 | tf_op jit(solution)/shard_map/all_to_all | solution.py:146
  15.6 2.8 %collective-permute-done = bf16[384,896]{1,0:T(8,128)(2,1)S(1)} collective-permute-done((bf16[384,896]{1,0:T(8,128)(2,1)S(1)}, bf16[384,896]{1,0:T(8,128)(2,1)S(1)}, u32[]{:S(2)}, u32[]{:S(2)}) %collective-permute-start) | collective-permute-done | bytes 688160 | tf_op jit(solution)/shard_map/ppermute | solution.py:129
  21.3 7.6 %all-to-all-start.2 = ((bf16[16,48,896]{2,1,0:T(8,128)(2,1)}), bf16[16,48,896]{2,1,0:T(8,128)(2,1)}, u32[]{:S(2)}, u32[]{:S(2)}) async-start(bf16[16,48,896]{2,1,0:T(8,128)(2,1)} %bitcast.45), calls=%async_computation.2 | async-start | bytes 2752512 | tf_op jit(solution)/shard_map/all_to_all | solution.py:225
  35.6 18.1 %collective-permute-done.1 = bf16[384,1280]{1,0:T(8,128)(2,1)S(1)} collective-permute-done((bf16[384,1280]{1,0:T(8,128)(2,1)S(1)}, bf16[384,1280]{1,0:T(8,128)(2,1)S(1)}, u32[]{:S(2)}, u32[]{:S(2)}) %collective-permute-start.1) | collective-permute-done | bytes 983072 | tf_op jit(solution)/shard_map/ppermute | solution.py:129
  57.2 3.3 %all-to-all-done.2 = bf16[16,48,896]{2,1,0:T(8,128)(2,1)} async-done(((bf16[16,48,896]{2,1,0:T(8,128)(2,1)}), bf16[16,48,896]{2,1,0:T(8,128)(2,1)}, u32[]{:S(2)}, u32[]{:S(2)}) %all-to-all-start.2) | async-done | bytes 1376288 | tf_op jit(solution)/shard_map/all_to_all | solution.py:225
  60.5 5.3 %all-to-all-start.1 = ((bf16[16,48,1280]{2,1,0:T(8,128)(2,1)}), bf16[16,48,1280]{2,1,0:T(8,128)(2,1)S(1)}, u32[]{:S(2)}, u32[]{:S(2)}) async-start(bf16[16,48,1280]{2,1,0:T(8,128)(2,1)} %bitcast.44), calls=%async_computation.1 | async-start | bytes 3932160 | tf_op jit(solution)/shard_map/all_to_all | solution.py:225
  66.0 2.8 %multiply_convert_fusion.5 = bf16[384,1920]{1,0:T(8,128)(2,1)} fusion(f32[1920]{0:T(1024)S(1)} %get-tuple-element.50, bf16[384,8192]{1,0:T(8,128)(2,1)} %param.6, s32[]{:T(128)S(6)} %select_n.118), kind=kLoop, calls=%fused_computation.21 | loop fusion | flops 2211840 | bytes 2956804 | tf_op jit(solution)/shard_map/convert_element_type | solution.py:159
  70.0 4.7 %convolution_convert_fusion.1 = bf16[768,1920]{1,0:T(8,128)(2,1)} fusion(f32[1920]{0:T(1024)S(1)} %get-tuple-element.51, bf16[384,8192]{1,0:T(8,128)(2,1)} %param.6, s32[]{:T(128)S(6)} %select_n.116, s32[384]{0:T(512)S(1)} %get-tuple-element.53), kind=kOutput, calls=%fused_computation.15 | convolution fusion | flops 1136443392 | bytes 4432900 | tf_op jit(solution)/shard_map/dot_general | solution.py:200
  74.7 9.0 %fusion.2 = f32[384,1024]{1,0:T(8,128)} fusion(bf16[8192,1024]{1,0:T(8,128)(2,1)} %param.8, f32[4096]{0:T(1024)S(1)} %get-tuple-element.44, bf16[384,8192]{1,0:T(8,128)(2,1)} %param.6), kind=kOutput, calls=%fused_computation.3 | convolution fusion | flops 3225944064 | bytes 13123584 | tf_op jit(solution)/shard_map/dot_general | solution.py:182
  83.7 18.9 %collective-permute-done.2 = bf16[384,1920]{1,0:T(8,128)(2,1)} collective-permute-done((bf16[384,1920]{1,0:T(8,128)(2,1)}, bf16[384,1920]{1,0:T(8,128)(2,1)}, u32[]{:S(2)}, u32[]{:S(2)}) %collective-permute-start.2) | collective-permute-done | bytes 1474592 | tf_op jit(solution)/shard_map/ppermute | solution.py:129
  102.6 4.8 %add_convert_fusion = bf16[768,1920]{1,0:T(8,128)(2,1)} fusion(bf16[768,1920]{1,0:T(8,128)(2,1)S(1)} %copy-done.18, bf16[384,1920]{1,0:T(8,128)(2,1)} %collective-permute-done.2, s32[384]{0:T(512)S(1)} %get-tuple-element.52), kind=kOutput, calls=%fused_computation.9 | convolution fusion | flops 1137180672 | bytes 7374336 | tf_op jit(solution)/shard_map/dot_general | solution.py:218
  110.5 6.2 %all-to-all-start = ((bf16[16,48,1920]{2,1,0:T(8,128)(2,1)}), bf16[16,48,1920]{2,1,0:T(8,128)(2,1)S(1)}, u32[]{:S(2)}, u32[]{:S(2)}) async-start(bf16[16,48,1920]{2,1,0:T(8,128)(2,1)} %bitcast.42), calls=%async_computation | async-start | bytes 5898240 | tf_op jit(solution)/shard_map/all_to_all | solution.py:225
  116.7 3.6 %multiply_convert_fusion.2 = bf16[384,3328]{1,0:T(8,128)(2,1)} fusion(f32[3328]{0:T(1024)S(1)} %bitcast.49, bf16[384,8192]{1,0:T(8,128)(2,1)} %param.6, s32[]{:T(128)S(6)} %select_n.122), kind=kLoop, calls=%fused_computation.10 | loop fusion | flops 3833856 | bytes 5125124 | tf_op jit(solution)/shard_map/convert_element_type | solution.py:159
  123.1 2.9 %slice.38.down_ref = bf16[512,1920]{1,0:T(8,128)(2,1)} slice(bf16[512,4096]{1,0:T(8,128)(2,1)} %bitcast.46), slice={[0:512], [2176:4096]} | slice | bytes 3932160 | tf_op jit(solution)/shard_map/slice | solution.py:240
  131.2 2.8 %fusion.15 = f32[384,1024]{1,0:T(8,128)S(1)} fusion(bf16[384,896]{1,0:T(8,128)(2,1)} %copy-done.17, bf16[8192,1024]{1,0:T(8,128)(2,1)} %param.8, s32[]{:T(128)S(6)} %select_n.120), kind=kOutput, calls=%fused_computation.28 | convolution fusion | flops 704643072 | bytes 4096004 | tf_op jit(solution)/shard_map/dot_general | solution.py:219
  134.0 2.9 %fusion.13 = f32[384,1024]{1,0:T(8,128)S(1)} fusion(bf16[384,1280]{1,0:T(8,128)(2,1)S(1)} %copy-done.16, bf16[8192,1024]{1,0:T(8,128)(2,1)} %param.8, s32[]{:T(128)S(6)} %select_n.119), kind=kOutput, calls=%fused_computation.24 | convolution fusion | flops 1006632960 | bytes 5177348 | tf_op jit(solution)/shard_map/dot_general | solution.py:219
  136.9 5.7 %add_add_fusion.1 = f32[384,1024]{1,0:T(8,128)} fusion(f32[384,1024]{1,0:T(8,128)S(1)} %fusion.15, f32[384,1024]{1,0:T(8,128)S(1)} %fusion.13, bf16[384,1920]{1,0:T(8,128)(2,1)} %collective-permute-done.2, bf16[8192,1024]{1,0:T(8,128)(2,1)} %param.8, s32[]{:T(128)S(6)} %select_n.116), kind=kOutput, calls=%fused_computation.37 | convolution fusion | flops 1510735872 | bytes 10125316 | tf_op jit(solution)/shard_map/dot_general | solution.py:219
  147.7 29.7 %collective-permute-done.3 = f32[384]{0:T(512)S(1)} collective-permute-done((f32[384]{0:T(512)S(1)}, f32[384]{0:T(512)S(1)}, u32[]{:S(2)}, u32[]{:S(2)}) %collective-permute-start.3) | collective-permute-done | bytes 1568 | tf_op jit(solution)/shard_map/ppermute | solution.py:129
  177.4 3.0 %all-to-all-done = bf16[16,48,1920]{2,1,0:T(8,128)(2,1)S(1)} async-done(((bf16[16,48,1920]{2,1,0:T(8,128)(2,1)}), bf16[16,48,1920]{2,1,0:T(8,128)(2,1)S(1)}, u32[]{:S(2)}, u32[]{:S(2)}) %all-to-all-start) | async-done | bytes 2949152 | tf_op jit(solution)/shard_map/all_to_all | solution.py:225
  186.4 7.7 %fusion.4 = f32[384,1024]{1,0:T(8,128)} fusion(bf16[384,3328]{1,0:T(8,128)(2,1)} %collective-permute-done.4, bf16[8192,1024]{1,0:T(8,128)(2,1)} %param.8, s32[]{:T(128)S(6)} %select_n.115), kind=kOutput, calls=%fused_computation.5 | convolution fusion | flops 2617245696 | bytes 10944516 | tf_op jit(solution)/shard_map/dot_general | solution.py:259
  196.5 7.2 %all-to-all-start.4 = ((bf16[16,48,512]{2,1,0:T(8,128)(2,1)}), bf16[16,48,512]{2,1,0:T(8,128)(2,1)S(1)}, u32[]{:S(2)}, u32[]{:S(2)}) async-start(bf16[16,48,512]{2,1,0:T(8,128)(2,1)} %bitcast.19), calls=%async_computation.4 | async-start | bytes 1572864 | tf_op jit(solution)/shard_map/all_to_all | solution.py:271
  205.2 6.9 %fusion = f32[384,1024]{1,0:T(8,128)S(1)} fusion(bf16[8192,1024]{1,0:T(8,128)(2,1)} %param.8, f32[4096]{0:T(1024)S(1)} %get-tuple-element.43, bf16[384,8192]{1,0:T(8,128)(2,1)} %param.6), kind=kOutput, calls=%fused_computation.1 | convolution fusion | flops 3225944064 | bytes 13123584 | tf_op jit(solution)/shard_map/dot_general | solution.py:182
  213.5 6.0 %collective-permute-done.6 = bf16[384,768]{1,0:T(8,128)(2,1)S(1)} collective-permute-done((bf16[384,768]{1,0:T(8,128)(2,1)S(1)}, bf16[384,768]{1,0:T(8,128)(2,1)S(1)}, u32[]{:S(2)}, u32[]{:S(2)}) %collective-permute-start.6) | collective-permute-done | bytes 589856 | tf_op jit(solution)/shard_map/ppermute | solution.py:129
  225.6 2.6 %shard_map.65 = bf16[768,1024]{1,0:T(8,128)(2,1)} custom-call(s32[2]{0:T(128)S(1)} %pad_add_fusion.owners_ref, s32[384,1]{1,0:T(8,128)S(1)} %copy-done.4, s32[384,1]{1,0:T(8,128)S(1)} %copy-done.5, f32[384,1]{1,0:T(8,128)S(1)} %copy-done.6, f32[384,1]{1,0:T(8,128)S(1)} %copy-done.7, f32[384,1024]{1,0:T(8,128)S(1)} %copy-done.2, ...), custom_call_target="tpu_custom_call" | custom-call | flops 603979776 | bytes 5505024 | tf_op jit(solution)/shard_map/pallas_call | solution.py:91
  (99 shorter events, 56.5 us)
Async XLA Ops:
  0.0 194.9 %copy-start = (bf16[8,64,512]{2,1,0:T(8,128)(2,1)S(1)}, bf16[8,64,512]{2,1,0:T(8,128)(2,1)}, u32[]{:S(2)}) copy-start(bf16[8,64,512]{2,1,0:T(8,128)(2,1)} %param.10) | copy-start | bytes 1572868
  2.1 16.4 %collective-permute-start = (bf16[384,896]{1,0:T(8,128)(2,1)S(1)}, bf16[384,896]{1,0:T(8,128)(2,1)S(1)}, u32[]{:S(2)}, u32[]{:S(2)}) collective-permute-start(bf16[384,896]{1,0:T(8,128)(2,1)S(1)} %multiply_convert_fusion.11), channel_id=1, source_target_pairs={{0,1},{1,0},{2,3},{3,2},{4,5},{5,4},{6,7},{7,6},{8,9},{9,8},{10,11... | collective-permute-start | bytes 2064392 | tf_op jit(solution)/shard_map/ppermute | solution.py:129
  5.7 15.6 %all-to-all-start.3 = ((s32[16,1,12]{2,1,0:T(1,128)}), s32[16,1,12]{2,1,0:T(1,128)S(1)}, u32[]{:S(2)}, u32[]{:S(2)}) async-start(s32[16,1,12]{2,1,0:T(1,128)} %bitcast.17), calls=%async_computation.3 | async-start | bytes 16384 | tf_op jit(solution)/shard_map/all_to_all | solution.py:146
  19.3 14.9 %slice-start = ((s8[6291456]{0:T(1024)(128)(4,1)}), s8[2097152]{0:T(1024)(128)(4,1)S(1)}, s32[]{:S(2)}) async-start(s8[6291456]{0:T(1024)(128)(4,1)} %bitcast.40), calls=%async_computation.5 | async-start | bytes 4194304
  21.3 7.6 %copy-start.14 = (bf16[8192]{0:T(1024)(128)(2,1)S(1)}, bf16[8192]{0:T(1024)(128)(2,1)}, u32[]{:S(2)}) copy-start(bf16[8192]{0:T(1024)(128)(2,1)} %param.7) | copy-start | bytes 49156
  21.3 39.2 %all-to-all-start.2 = ((bf16[16,48,896]{2,1,0:T(8,128)(2,1)}), bf16[16,48,896]{2,1,0:T(8,128)(2,1)}, u32[]{:S(2)}, u32[]{:S(2)}) async-start(bf16[16,48,896]{2,1,0:T(8,128)(2,1)} %bitcast.45), calls=%async_computation.2 | async-start | bytes 2752512 | tf_op jit(solution)/shard_map/all_to_all | solution.py:225
  29.0 5.2 %slice-start.1 = ((s8[6291456]{0:T(1024)(128)(4,1)}), s8[4194304]{0:T(1024)(128)(4,1)S(1)}, s32[]{:S(2)}) async-start(s8[6291456]{0:T(1024)(128)(4,1)} %bitcast.40), calls=%async_computation.6 | async-start | bytes 8388608
  30.5 23.1 %collective-permute-start.1 = (bf16[384,1280]{1,0:T(8,128)(2,1)S(1)}, bf16[384,1280]{1,0:T(8,128)(2,1)S(1)}, u32[]{:S(2)}, u32[]{:S(2)}) collective-permute-start(bf16[384,1280]{1,0:T(8,128)(2,1)S(1)} %multiply_convert_fusion.8), channel_id=1, source_target_pairs={{0,1},{1,0},{2,3},{3,2},{4,5},{5,4},{6,7},{7,6},{8,9},{9,8},{10,11... | collective-permute-start | bytes 2949128 | tf_op jit(solution)/shard_map/ppermute | solution.py:129
  60.5 48.7 %all-to-all-start.1 = ((bf16[16,48,1280]{2,1,0:T(8,128)(2,1)}), bf16[16,48,1280]{2,1,0:T(8,128)(2,1)S(1)}, u32[]{:S(2)}, u32[]{:S(2)}) async-start(bf16[16,48,1280]{2,1,0:T(8,128)(2,1)} %bitcast.44), calls=%async_computation.1 | async-start | bytes 3932160 | tf_op jit(solution)/shard_map/all_to_all | solution.py:225
  68.7 33.8 %collective-permute-start.2 = (bf16[384,1920]{1,0:T(8,128)(2,1)}, bf16[384,1920]{1,0:T(8,128)(2,1)}, u32[]{:S(2)}, u32[]{:S(2)}) collective-permute-start(bf16[384,1920]{1,0:T(8,128)(2,1)} %multiply_convert_fusion.5), channel_id=1, source_target_pairs={{0,1},{1,0},{2,3},{3,2},{4,5},{5,4},{6,7},{7,6},{8,9},{9,8},{10,11... | collective-permute-start | bytes 4423688 | tf_op jit(solution)/shard_map/ppermute | solution.py:129
  74.7 27.9 %copy-start.18 = (bf16[768,1920]{1,0:T(8,128)(2,1)S(1)}, bf16[768,1920]{1,0:T(8,128)(2,1)}, u32[]{:S(2)}) copy-start(bf16[768,1920]{1,0:T(8,128)(2,1)} %convolution_convert_fusion.1) | copy-start | bytes 8847364
  110.5 69.8 %all-to-all-start = ((bf16[16,48,1920]{2,1,0:T(8,128)(2,1)}), bf16[16,48,1920]{2,1,0:T(8,128)(2,1)S(1)}, u32[]{:S(2)}, u32[]{:S(2)}) async-start(bf16[16,48,1920]{2,1,0:T(8,128)(2,1)} %bitcast.42), calls=%async_computation | async-start | bytes 5898240 | tf_op jit(solution)/shard_map/all_to_all | solution.py:225
  120.3 57.0 %collective-permute-start.4 = (bf16[384,3328]{1,0:T(8,128)(2,1)}, bf16[384,3328]{1,0:T(8,128)(2,1)}, u32[]{:S(2)}, u32[]{:S(2)}) collective-permute-start(bf16[384,3328]{1,0:T(8,128)(2,1)} %multiply_convert_fusion.2), channel_id=1, source_target_pairs={{0,1},{1,0},{2,3},{3,2},{4,5},{5,4},{6,7},{7,6},{8,9},{9,8},{10,11... | collective-permute-start | bytes 7667720 | tf_op jit(solution)/shard_map/ppermute | solution.py:129
  130.1 47.3 %collective-permute-start.3 = (f32[384]{0:T(512)S(1)}, f32[384]{0:T(512)S(1)}, u32[]{:S(2)}, u32[]{:S(2)}) collective-permute-start(f32[384]{0:T(512)S(1)} %add_rsqrt_fusion), channel_id=1, source_target_pairs={{0,1},{1,0},{2,3},{3,2},{4,5},{5,4},{6,7},{7,6},{8,9},{9,8},{10,11... | collective-permute-start | bytes 4616 | tf_op jit(solution)/shard_map/ppermute | solution.py:129
  136.9 5.8 %copy-start.13 = (bf16[8,4096,64]{1,2,0:T(8,128)(2,1)S(1)}, bf16[8,4096,64]{1,2,0:T(8,128)(2,1)}, u32[]{:S(2)}) copy-start(bf16[8,4096,64]{1,2,0:T(8,128)(2,1)} %param.9) | copy-start | bytes 12582916
  185.1 9.8 %collective-permute-start.5 = (f32[64,768]{1,0:T(8,128)S(1)}, f32[64,768]{1,0:T(8,128)S(1)}, u32[]{:S(2)}, u32[]{:S(2)}) collective-permute-start(f32[64,768]{1,0:T(8,128)S(1)} %shard_map.64), channel_id=1, source_target_pairs={{0,1},{1,0},{2,3},{3,2},{4,5},{5,4},{6,7},{7,6},{8,9},{9,8},{10,11... | collective-permute-start | bytes 589832 | tf_op jit(solution)/shard_map/ppermute | solution.py:129
  196.5 26.8 %all-to-all-start.4 = ((bf16[16,48,512]{2,1,0:T(8,128)(2,1)}), bf16[16,48,512]{2,1,0:T(8,128)(2,1)S(1)}, u32[]{:S(2)}, u32[]{:S(2)}) async-start(bf16[16,48,512]{2,1,0:T(8,128)(2,1)} %bitcast.19), calls=%async_computation.4 | async-start | bytes 1572864 | tf_op jit(solution)/shard_map/all_to_all | solution.py:271
  204.9 14.6 %collective-permute-start.6 = (bf16[384,768]{1,0:T(8,128)(2,1)S(1)}, bf16[384,768]{1,0:T(8,128)(2,1)S(1)}, u32[]{:S(2)}, u32[]{:S(2)}) collective-permute-start(bf16[384,768]{1,0:T(8,128)(2,1)S(1)} %multiply_convert_fusion.12), channel_id=1, source_target_pairs={{0,1},{1,0},{2,3},{3,2},{4,5},{5,4},{6,7},{7,6},{8,9},{9,8},{10,11... | collective-permute-start | bytes 1769480 | tf_op jit(solution)/shard_map/ppermute | solution.py:129
  205.2 6.9 %copy-start.12 = (f32[384,1024]{1,0:T(8,128)S(1)}, f32[384,1024]{1,0:T(8,128)}, u32[]{:S(2)}) copy-start(f32[384,1024]{1,0:T(8,128)} %fusion.2) | copy-start | bytes 4718596
  212.1 7.4 %copy-start.8 = (f32[384,1024]{1,0:T(8,128)S(1)}, f32[384,1024]{1,0:T(8,128)}, u32[]{:S(2)}) copy-start(f32[384,1024]{1,0:T(8,128)} %add_add_fusion.1) | copy-start | bytes 4718596
  212.1 7.4 %copy-start.9 = (f32[384,1024]{1,0:T(8,128)S(1)}, f32[384,1024]{1,0:T(8,128)}, u32[]{:S(2)}) copy-start(f32[384,1024]{1,0:T(8,128)} %fusion.4) | copy-start | bytes 4718596
  213.5 9.7 %copy-start.4 = (s32[384,1]{1,0:T(8,128)S(1)}, s32[384,1]{1,0:T(8,128)}, u32[]{:S(2)}) copy-start(s32[384,1]{1,0:T(8,128)} %broadcast_in_dim.74.refs_0_) | copy-start | bytes 4612
  213.5 9.7 %copy-start.5 = (s32[384,1]{1,0:T(8,128)S(1)}, s32[384,1]{1,0:T(8,128)}, u32[]{:S(2)}) copy-start(s32[384,1]{1,0:T(8,128)} %broadcast_in_dim.75.refs_1_) | copy-start | bytes 4612
  213.5 9.7 %copy-start.6 = (f32[384,1]{1,0:T(8,128)S(1)}, f32[384,1]{1,0:T(8,128)}, u32[]{:S(2)}) copy-start(f32[384,1]{1,0:T(8,128)} %rsqrt.15.refs_2_) | copy-start | bytes 4612
  (9 other events, 13.8 us)

commit v5 on v4

--- a/solution.py
+++ b/solution.py
@@ -34,34 +34,51 @@
     return lax.dynamic_slice_in_dim(rows, start, width, 1)
 
 
-def shrink_kernel(adapters, down_ref, sent_ref, earlier_ref, slot_adapter_ref, out_ref):
+def shrink_kernel(adapters, down_ref, sent_ref, earlier_ref, slot_adapter_ref, out_ref, total_ref):
     rank_width, slots = out_ref.shape
     step = 256 if slots % 256 == 0 else slots
+    part = pl.program_id(0)
+
+    @pl.when(part == 0)
+    def _():
+        total_ref[...] = earlier_ref[...]
+
     for start in range(0, slots, step):
         columns = slice(start, start + step)
-        partial_value = earlier_ref[:, columns] + lax.dot_general(
+        total_ref[:, columns] += lax.dot_general(
             down_ref[...],
             sent_ref[columns, :],
             (((1,), (1,)), ((), ())),
             preferred_element_type=jnp.float32,
         )
-        named = slot_adapter_ref[:, columns]
-        chosen = jnp.zeros((rank_width, step), jnp.float32)
+
+    @pl.when(part == pl.num_programs(0) - 1)
+    def _():
+        named = slot_adapter_ref[...]
+        chosen = jnp.zeros((rank_width, slots), jnp.float32)
         for adapter in range(adapters):
-            rows = partial_value[adapter * rank_width : (adapter + 1) * rank_width]
+            rows = total_ref[adapter * rank_width : (adapter + 1) * rank_width, :]
             chosen = jnp.where(named == adapter, rows, chosen)
-        out_ref[:, columns] = chosen
+        out_ref[...] = chosen
 
 
 def shrink_last(down, sent, earlier, slot_adapter, adapters):
     rows, width = down.shape
     slots = sent.shape[0]
+    tile = next(size for size in (640, 512, 384, 256, 128) if width % size == 0)
     return pl.pallas_call(
         functools.partial(shrink_kernel, adapters),
         out_shape=jax.ShapeDtypeStruct((rows // adapters, slots), jnp.float32),
-        in_specs=[pl.BlockSpec(memory_space=pltpu.VMEM)] * 4,
-        out_specs=pl.BlockSpec(memory_space=pltpu.VMEM),
-        compiler_params=pltpu.CompilerParams(vmem_limit_bytes=16 * 1024 * 1024),
+        grid=(width // tile,),
+        in_specs=[
+            pl.BlockSpec((rows, tile), lambda k: (0, k)),
+            pl.BlockSpec((slots, tile), lambda k: (0, k)),
+            pl.BlockSpec((rows, slots), lambda k: (0, 0)),
+            pl.BlockSpec((1, slots), lambda k: (0, 0)),
+        ],
+        out_specs=pl.BlockSpec((rows // adapters, slots), lambda k: (0, 0)),
+        scratch_shapes=[pltpu.VMEM((rows, slots), jnp.float32)],
+        compiler_params=pltpu.CompilerParams(vmem_limit_bytes=20 * 1024 * 1024),
         cost_estimate=pl.CostEstimate(
             flops=2 * rows * width * slots,
             bytes_accessed=(rows + slots) * width * 2 + rows * slots * 4,
@@ -74,27 +91,46 @@
     slots, factors, bases = refs[:count], refs[count : 2 * count], refs[2 * count : 3 * count]
     returned_ref, out_ref = refs[3 * count :]
     rows, width = bases[0].shape
-    half = width // 2
-    for i in range(count):
-        slot = lax.broadcasted_iota(jnp.int32, (rows, returned_ref.shape[0]), 1)
-        take = jnp.where(slot == slots[i][...], 1.0, 0.0).astype(jnp.bfloat16)
-        delta = jnp.dot(take, returned_ref[...], preferred_element_type=jnp.float32)
-        factor = factors[i][...]
-        place = pl.ds(pl.multiple_of(owners_ref[i] * rows, rows), rows)
-        out_ref[place, :half] = (bases[i][:, :half] * factor).astype(out_ref.dtype)
-        out_ref[place, half:] = ((bases[i][:, half:] + delta) * factor).astype(out_ref.dtype)
+    half = returned_ref.shape[1]
+
+    def place(i):
+        return pl.ds(pl.multiple_of(owners_ref[i] * rows, rows), rows)
+
+    def keys():
+        for i in range(count):
+            out_ref[place(i), :half] = (bases[i][:, :half] * factors[i][...]).astype(out_ref.dtype)
+
+    def vals():
+        for i in range(count):
+            slot = lax.broadcasted_iota(jnp.int32, (rows, returned_ref.shape[0]), 1)
+            take = jnp.where(slot == slots[i][...], 1.0, 0.0).astype(jnp.bfloat16)
+            delta = jnp.dot(take, returned_ref[...], preferred_element_type=jnp.float32)
+            value = (bases[i][:, width - half :] + delta) * factors[i][...]
+            out_ref[place(i), width - half :] = value.astype(out_ref.dtype)
+
+    if width == half:
+        pl.when(pl.program_id(0) == 0)(keys)
+        pl.when(pl.program_id(0) == 1)(vals)
+    else:
+        keys()
+        vals()
 
 
 def finish(owners, slots, factors, bases, returned):
     count = len(bases)
     rows, width = bases[0].shape
+    block = width // 2 if width // 2 % 128 == 0 else width
+    whole = lambda shape: pl.BlockSpec(shape, lambda j: (0, 0))
     return pl.pallas_call(
         functools.partial(finish_kernel, count),
         out_shape=jax.ShapeDtypeStruct((rows * count, width), jnp.bfloat16),
+        grid=(width // block,),
         in_specs=[pl.BlockSpec(memory_space=pltpu.SMEM)]
-        + [pl.BlockSpec(memory_space=pltpu.VMEM)] * (3 * count + 1),
-        out_specs=pl.BlockSpec(memory_space=pltpu.VMEM),
-        compiler_params=pltpu.CompilerParams(vmem_limit_bytes=16 * 1024 * 1024),
+        + [whole((rows, 1))] * (2 * count)
+        + [pl.BlockSpec((rows, block), lambda j: (0, j))] * count
+        + [whole(returned.shape)],
+        out_specs=pl.BlockSpec((rows * count, block), lambda j: (0, j)),
+        compiler_params=pltpu.CompilerParams(vmem_limit_bytes=20 * 1024 * 1024),
         cost_estimate=pl.CostEstimate(
             flops=2 * rows * count * returned.shape[0] * returned.shape[1],
             bytes_accessed=rows * count * width * 6 + returned.size * 2,
@@ -193,6 +229,7 @@
     ]
     own, inverse, gate = None, [], ()
     partials = []
+    count = len(offsets)
     for part, (low, high) in enumerate(bounds):
         width = high - low
         sending[part] = [after(piece, *gate) for piece in sending[part]]
@@ -209,9 +246,10 @@
             values = after(later_rows, *gate).astype(jnp.float32)
             inverse = [lax.rsqrt(jnp.mean(values * values, axis=-1) + EPS)]
             inverse += [to_offset(inverse[0], offset) for offset in offsets]
-            pieces = [after(piece, inverse[0]) for piece in pieces]
+            own = own_product(after(later_rows, *gate), 0, model_width // 4)
+            own, *pieces = lax.optimization_barrier((own, *pieces, inverse[0]))[: count + 1]
         else:
-            own = own_product(after(later_rows, *gate), 0, model_width // 2)
+            own += own_product(after(later_rows, *gate), model_width // 4, model_width * 3 // 4)
             own, *pieces = lax.optimization_barrier((own, *pieces))
         gate = pieces
         for offset, piece in zip(offsets, pieces):
@@ -239,7 +277,6 @@
     sent, earlier_sum, last_down, *tied = lax.optimization_barrier(
         (sent, partials[-1], down[:, low:high], *others, *inverse[1:], *early)
     )
-    count = len(offsets)
     others, inverse[1:], early = tied[:count], tied[count : 2 * count], tied[2 * count :]
     partial_value = shrink_last(last_down, sent, earlier_sum, slot_adapter[None, :], resident_adapters)
     total = partial_value
@@ -248,7 +285,8 @@
 
     weight_rows = rest_weight()
     last_rows = after(later_rows, total)
-    own += own_product(last_rows, model_width // 2, model_width)
+    own += own_product(last_rows, model_width * 3 // 4, model_width)
+    early = [after(piece, total) for piece in early]
     for offset in offsets:
         late = to_offset(rest_of(offset, last_rows)[:, rest_cut:], offset)
         late, own = lax.optimization_barrier((late, own))

time: 230 us -> 232 us (level)
  waiting for transfers between devices: 85.1 us -> 81.7 us
  starting transfers between devices: 40.2 us -> 43 us
    ppermute x7, waiting for transfers between devices: 75.5 us -> 70.6 us  [to_offset(): return lax.ppermute(value, 'tensor', pairs)]
    all_to_all x1, waiting for transfers between devices: 1.51 us -> 5.21 us  [per_device(): lax.all_to_all(correction.reshape(adapter_count, holder_slots, column_blo...]
    unnamed x42 -> x40, local copies, waits for them, and re-layouts: 8.55 us -> 7.69 us
    dot_general x2 -> x3, matrix products: 15.9 us -> 16.6 us  [own_product(): jnp.dot(scaled(rows, low, high - low), key_value_weight[low:high], prefer...]
  transfers between devices with their start and end apart: 12 -> 12, of which waited for: 9 -> 9; matrix products, arithmetic and copies ran while one was open for 38% -> 39% of each run, Pallas kernels for 0% -> 0%
where the time goes in v5:
time: 232 us; the launch traced here: 230 us
  waiting for transfers between devices  81.7 us (35%)
  matrix products  64 us (28%)
  starting transfers between devices  43 us (19%)
  other arithmetic  18.5 us (8%)
  local copies, waits for them, and re-layouts  17.3 us (7%)
  Pallas kernels  5.74 us (2%)
    ppermute x7, waiting for transfers between devices, to_offset(): return lax.ppermute(value, 'tensor', pairs)  70.6 us
    all_to_all x3, starting transfers between devices, per_device(): lax.all_to_all(outgoing, 'adapter', split_axis=0, concat_axis=0, tiled=True)  19.5 us
    dot_general x3, matrix products, own_product(): jnp.dot(scaled(rows, low, high - low), key_value_weight[low:high], prefer...  16.6 us
    dot_general x3, matrix products, per_device(): jnp.dot(piece, lax.dynamic_slice_in_dim(key_value_weight, own_start + low...  11.4 us
    dot_general x3, matrix products, per_device(): jnp.dot(place[offset], piece, preferred_element_type=jnp.float32)  10.9 us
    dot_general x3, matrix products, per_device(): jnp.dot(place[0], scaled(residual_rows if part == 0 else later_rows, own_...  10.4 us
    convert_element_type x5, other arithmetic, scaled(): (features(rows, start, width).astype(jnp.float32) * gain).astype(jnp.bflo...  10.2 us
    all_to_all x1, starting transfers between devices, per_device(): lax.all_to_all(correction.reshape(adapter_count, holder_slots, column_blo...  8.81 us
  transfers between devices with their start and end apart: 12, of which 9 were waited for; matrix products, arithmetic and copies ran while one was open for 39% of the time, Pallas kernels for 0%

profile of v5, /device:TPU:9, one launch (start us, length us, event | category | flops | bytes accessed | tf_op | source)
XLA Modules:
  0.0 230.5 jit_solution(7688470465066404825)
XLA Ops:
  5.7 6.9 %all-to-all-start.3 = ((s32[16,1,12]{2,1,0:T(1,128)}), s32[16,1,12]{2,1,0:T(1,128)S(1)}, u32[]{:S(2)}, u32[]{:S(2)}) async-start(s32[16,1,12]{2,1,0:T(1,128)} %bitcast.17), calls=%async_computation.3 | async-start | bytes 16384 | tf_op jit(solution)/shard_map/all_to_all | solution.py:182
  13.6 3.1 %convolution_convert_fusion.2 = bf16[768,896]{1,0:T(8,128)(2,1)} fusion(f32[896]{0:T(1024)S(1)} %get-tuple-element.53, bf16[384,8192]{1,0:T(8,128)(2,1)} %param.6, s32[]{:T(128)S(6)} %select_n.120, s32[384]{0:T(512)S(1)} %get-tuple-element.58), kind=kOutput, calls=%fused_computation.31 | convolution fusion | flops 530497536 | bytes 2069508 | tf_op jit(solution)/shard_map/dot_general | solution.py:237
  18.4 3.6 %add_convert_fusion.1 = bf16[768,896]{1,0:T(8,128)(2,1)} fusion(bf16[768,896]{1,0:T(8,128)(2,1)} %convolution_convert_fusion.2, bf16[384,896]{1,0:T(8,128)(2,1)S(1)} %collective-permute-done, s32[384]{0:T(512)S(1)} %get-tuple-element.57), kind=kOutput, calls=%fused_computation.24 | convolution fusion | flops 530841600 | bytes 3442176 | tf_op jit(solution)/shard_map/dot_general | solution.py:256
  22.1 7.5 %all-to-all-start.2 = ((bf16[16,48,896]{2,1,0:T(8,128)(2,1)}), bf16[16,48,896]{2,1,0:T(8,128)(2,1)}, u32[]{:S(2)}, u32[]{:S(2)}) async-start(bf16[16,48,896]{2,1,0:T(8,128)(2,1)} %bitcast.45), calls=%async_computation.2 | async-start | bytes 2752512 | tf_op jit(solution)/shard_map/all_to_all | solution.py:263
  36.2 5.1 %fusion.6 = f32[384,1024]{1,0:T(8,128)} fusion(bf16[8192,1024]{1,0:T(8,128)(2,1)} %param.8, f32[2048]{0:T(1024)S(1)} %get-tuple-element.48, bf16[384,8192]{1,0:T(8,128)(2,1)S(1)} %bitcast.41), kind=kOutput, calls=%fused_computation.10 | convolution fusion | flops 1612972032 | bytes 7348224 | tf_op jit(solution)/shard_map/dot_general | solution.py:218
  41.3 15.3 %collective-permute-done.1 = bf16[384,1280]{1,0:T(8,128)(2,1)S(1)} collective-permute-done((bf16[384,1280]{1,0:T(8,128)(2,1)S(1)}, bf16[384,1280]{1,0:T(8,128)(2,1)S(1)}, u32[]{:S(2)}, u32[]{:S(2)}) %collective-permute-start.1) | collective-permute-done | bytes 983072 | tf_op jit(solution)/shard_map/ppermute | solution.py:165
  61.2 5.8 %all-to-all-start.1 = ((bf16[16,48,1280]{2,1,0:T(8,128)(2,1)}), bf16[16,48,1280]{2,1,0:T(8,128)(2,1)S(1)}, u32[]{:S(2)}, u32[]{:S(2)}) async-start(bf16[16,48,1280]{2,1,0:T(8,128)(2,1)} %bitcast.44), calls=%async_computation.1 | async-start | bytes 3932160 | tf_op jit(solution)/shard_map/all_to_all | solution.py:263
  71.1 4.7 %convolution_convert_fusion.1 = bf16[768,1920]{1,0:T(8,128)(2,1)} fusion(f32[1920]{0:T(1024)S(1)} %get-tuple-element.56, bf16[384,8192]{1,0:T(8,128)(2,1)} %param.6, s32[]{:T(128)S(6)} %select_n.116, s32[384]{0:T(512)S(1)} %get-tuple-element.58), kind=kOutput, calls=%fused_computation.16 | convolution fusion | flops 1136443392 | bytes 4432900 | tf_op jit(solution)/shard_map/dot_general | solution.py:237
  75.8 6.9 %fusion = f32[384,1024]{1,0:T(8,128)S(1)} fusion(bf16[8192,1024]{1,0:T(8,128)(2,1)} %param.8, f32[4096]{0:T(1024)S(1)} %get-tuple-element.50, bf16[384,8192]{1,0:T(8,128)(2,1)} %param.6), kind=kOutput, calls=%fused_computation.1 | convolution fusion | flops 3225944064 | bytes 13123584 | tf_op jit(solution)/shard_map/dot_general | solution.py:218
  84.1 19.6 %collective-permute-done.2 = bf16[384,1920]{1,0:T(8,128)(2,1)} collective-permute-done((bf16[384,1920]{1,0:T(8,128)(2,1)}, bf16[384,1920]{1,0:T(8,128)(2,1)}, u32[]{:S(2)}, u32[]{:S(2)}) %collective-permute-start.2) | collective-permute-done | bytes 1474592 | tf_op jit(solution)/shard_map/ppermute | solution.py:165
  103.7 4.7 %add_convert_fusion = bf16[768,1920]{1,0:T(8,128)(2,1)} fusion(bf16[768,1920]{1,0:T(8,128)(2,1)S(1)} %copy-done.17, bf16[384,1920]{1,0:T(8,128)(2,1)} %collective-permute-done.2, s32[384]{0:T(512)S(1)} %get-tuple-element.57), kind=kOutput, calls=%fused_computation.6 | convolution fusion | flops 1137180672 | bytes 7374336 | tf_op jit(solution)/shard_map/dot_general | solution.py:256
  111.7 6.2 %all-to-all-start = ((bf16[16,48,1920]{2,1,0:T(8,128)(2,1)}), bf16[16,48,1920]{2,1,0:T(8,128)(2,1)S(1)}, u32[]{:S(2)}, u32[]{:S(2)}) async-start(bf16[16,48,1920]{2,1,0:T(8,128)(2,1)} %bitcast.42), calls=%async_computation | async-start | bytes 5898240 | tf_op jit(solution)/shard_map/all_to_all | solution.py:263
  117.8 3.6 %multiply_convert_fusion.1 = bf16[384,3328]{1,0:T(8,128)(2,1)} fusion(f32[3328]{0:T(1024)S(1)} %bitcast.49, bf16[384,8192]{1,0:T(8,128)(2,1)} %param.6, s32[]{:T(128)S(6)} %select_n.122), kind=kLoop, calls=%fused_computation.7 | loop fusion | flops 3833856 | bytes 5125124 | tf_op jit(solution)/shard_map/convert_element_type | solution.py:195
  124.3 2.9 %slice.42.down_ref = bf16[512,1920]{1,0:T(8,128)(2,1)} slice(bf16[512,4096]{1,0:T(8,128)(2,1)} %bitcast.46), slice={[0:512], [2176:4096]} | slice | bytes 3932160 | tf_op jit(solution)/shard_map/slice | solution.py:278
  134.2 2.9 %fusion.13 = f32[384,1024]{1,0:T(8,128)S(1)} fusion(bf16[384,1280]{1,0:T(8,128)(2,1)S(1)} %copy-done.15, bf16[8192,1024]{1,0:T(8,128)(2,1)} %param.8, s32[]{:T(128)S(6)} %select_n.119), kind=kOutput, calls=%fused_computation.25 | convolution fusion | flops 1006632960 | bytes 5177348 | tf_op jit(solution)/shard_map/dot_general | solution.py:257
  137.2 5.7 %add_add_fusion.1 = f32[384,1024]{1,0:T(8,128)} fusion(f32[384,1024]{1,0:T(8,128)S(1)} %fusion.15, f32[384,1024]{1,0:T(8,128)S(1)} %fusion.13, bf16[384,1920]{1,0:T(8,128)(2,1)} %collective-permute-done.2, bf16[8192,1024]{1,0:T(8,128)(2,1)} %param.8, s32[]{:T(128)S(6)} %select_n.116), kind=kOutput, calls=%fused_computation.40 | convolution fusion | flops 1510735872 | bytes 10125316 | tf_op jit(solution)/shard_map/dot_general | solution.py:257
  147.9 30.6 %collective-permute-done.3 = f32[384]{0:T(512)S(1)} collective-permute-done((f32[384]{0:T(512)S(1)}, f32[384]{0:T(512)S(1)}, u32[]{:S(2)}, u32[]{:S(2)}) %collective-permute-start.3) | collective-permute-done | bytes 1568 | tf_op jit(solution)/shard_map/ppermute | solution.py:165
  178.5 3.0 %all-to-all-done = bf16[16,48,1920]{2,1,0:T(8,128)(2,1)S(1)} async-done(((bf16[16,48,1920]{2,1,0:T(8,128)(2,1)}), bf16[16,48,1920]{2,1,0:T(8,128)(2,1)S(1)}, u32[]{:S(2)}, u32[]{:S(2)}) %all-to-all-start) | async-done | bytes 2949152 | tf_op jit(solution)/shard_map/all_to_all | solution.py:263
  184.4 3.1 %shard_map.64 = f32[64,768]{1,0:T(8,128)S(1)} custom-call(bf16[512,1920]{1,0:T(8,128)(2,1)S(1)} %copy-done.1, bf16[768,1920]{1,0:T(8,128)(2,1)S(1)} %bitcast.38, f32[512,768]{1,0:T(8,128)S(1)} %copy-done.3, s32[1,768]{1,0:T(1,128)S(1)} %broadcast_in_dim_reshape.4.slot_adapter_ref), custom_call_target="tpu_custom_call" | custom-call | flops 1509949440 | bytes 6488064 | tf_op jit(solution)/shard_map/pallas_call | solution.py:69
  189.7 3.4 %collective-permute-done.5 = f32[64,768]{1,0:T(8,128)S(1)} collective-permute-done((f32[64,768]{1,0:T(8,128)S(1)}, f32[64,768]{1,0:T(8,128)S(1)}, u32[]{:S(2)}, u32[]{:S(2)}) %collective-permute-start.5) | collective-permute-done | bytes 196640 | tf_op jit(solution)/shard_map/ppermute | solution.py:165
  197.2 8.8 %all-to-all-start.4 = ((bf16[16,48,512]{2,1,0:T(8,128)(2,1)}), bf16[16,48,512]{2,1,0:T(8,128)(2,1)S(1)}, u32[]{:S(2)}, u32[]{:S(2)}) async-start(bf16[16,48,512]{2,1,0:T(8,128)(2,1)} %bitcast.19), calls=%async_computation.4 | async-start | bytes 1572864 | tf_op jit(solution)/shard_map/all_to_all | solution.py:309
  206.0 4.6 %fusion.4 = f32[384,1024]{1,0:T(8,128)S(1)} fusion(bf16[8192,1024]{1,0:T(8,128)(2,1)} %param.8, f32[2048]{0:T(1024)S(1)} %get-tuple-element.47, bf16[384,8192]{1,0:T(8,128)(2,1)} %param.6), kind=kOutput, calls=%fused_computation.8 | convolution fusion | flops 1612972032 | bytes 7348224 | tf_op jit(solution)/shard_map/dot_general | solution.py:218
  212.0 5.9 %fusion.2 = f32[384,1024]{1,0:T(8,128)S(1)} fusion(bf16[384,3328]{1,0:T(8,128)(2,1)} %collective-permute-done.4, bf16[8192,1024]{1,0:T(8,128)(2,1)} %param.8, s32[]{:T(128)S(6)} %select_n.115), kind=kOutput, calls=%fused_computation.3 | convolution fusion | flops 2617245696 | bytes 10944516 | tf_op jit(solution)/shard_map/dot_general | solution.py:297
  220.3 5.2 %all-to-all-done.4 = bf16[16,48,512]{2,1,0:T(8,128)(2,1)S(1)} async-done(((bf16[16,48,512]{2,1,0:T(8,128)(2,1)}), bf16[16,48,512]{2,1,0:T(8,128)(2,1)S(1)}, u32[]{:S(2)}, u32[]{:S(2)}) %all-to-all-start.4) | async-done | bytes 786464 | tf_op jit(solution)/shard_map/all_to_all | solution.py:309
  (100 shorter events, 60.9 us)
Async XLA Ops:
  0.0 195.6 %copy-start = (bf16[8,64,512]{2,1,0:T(8,128)(2,1)S(1)}, bf16[8,64,512]{2,1,0:T(8,128)(2,1)}, u32[]{:S(2)}) copy-start(bf16[8,64,512]{2,1,0:T(8,128)(2,1)} %param.10) | copy-start | bytes 1572868
  0.8 15.9 %copy-start.13 = (bf16[8192]{0:T(1024)(128)(2,1)S(1)}, bf16[8192]{0:T(1024)(128)(2,1)}, u32[]{:S(2)}) copy-start(bf16[8192]{0:T(1024)(128)(2,1)} %param.7) | copy-start | bytes 49156
  2.1 16.4 %collective-permute-start = (bf16[384,896]{1,0:T(8,128)(2,1)S(1)}, bf16[384,896]{1,0:T(8,128)(2,1)S(1)}, u32[]{:S(2)}, u32[]{:S(2)}) collective-permute-start(bf16[384,896]{1,0:T(8,128)(2,1)S(1)} %multiply_convert_fusion.13), channel_id=1, source_target_pairs={{0,1},{1,0},{2,3},{3,2},{4,5},{5,4},{6,7},{7,6},{8,9},{9,8},{10,11... | collective-permute-start | bytes 2064392 | tf_op jit(solution)/shard_map/ppermute | solution.py:165
  5.7 16.4 %all-to-all-start.3 = ((s32[16,1,12]{2,1,0:T(1,128)}), s32[16,1,12]{2,1,0:T(1,128)S(1)}, u32[]{:S(2)}, u32[]{:S(2)}) async-start(s32[16,1,12]{2,1,0:T(1,128)} %bitcast.17), calls=%async_computation.3 | async-start | bytes 16384 | tf_op jit(solution)/shard_map/all_to_all | solution.py:182
  18.4 3.7 %copy-start.16 = (bf16[384,896]{1,0:T(8,128)(2,1)}, bf16[384,896]{1,0:T(8,128)(2,1)S(1)}, u32[]{:S(2)}) copy-start(bf16[384,896]{1,0:T(8,128)(2,1)S(1)} %collective-permute-done) | copy-start | bytes 2064388
  18.4 16.4 %slice-start = ((s8[6291456]{0:T(1024)(128)(4,1)}), s8[2097152]{0:T(1024)(128)(4,1)S(1)}, s32[]{:S(2)}) async-start(s8[6291456]{0:T(1024)(128)(4,1)} %bitcast.40), calls=%async_computation.5 | async-start | bytes 4194304
  22.1 39.1 %all-to-all-start.2 = ((bf16[16,48,896]{2,1,0:T(8,128)(2,1)}), bf16[16,48,896]{2,1,0:T(8,128)(2,1)}, u32[]{:S(2)}, u32[]{:S(2)}) async-start(bf16[16,48,896]{2,1,0:T(8,128)(2,1)} %bitcast.45), calls=%async_computation.2 | async-start | bytes 2752512 | tf_op jit(solution)/shard_map/all_to_all | solution.py:263
  29.6 5.2 %slice-start.1 = ((s8[6291456]{0:T(1024)(128)(4,1)}), s8[4194304]{0:T(1024)(128)(4,1)S(1)}, s32[]{:S(2)}) async-start(s8[6291456]{0:T(1024)(128)(4,1)} %bitcast.40), calls=%async_computation.6 | async-start | bytes 8388608
  33.5 23.0 %collective-permute-start.1 = (bf16[384,1280]{1,0:T(8,128)(2,1)S(1)}, bf16[384,1280]{1,0:T(8,128)(2,1)S(1)}, u32[]{:S(2)}, u32[]{:S(2)}) collective-permute-start(bf16[384,1280]{1,0:T(8,128)(2,1)S(1)} %multiply_convert_fusion.8), channel_id=1, source_target_pairs={{0,1},{1,0},{2,3},{3,2},{4,5},{5,4},{6,7},{7,6},{8,9},{9,8},{10,11... | collective-permute-start | bytes 2949128 | tf_op jit(solution)/shard_map/ppermute | solution.py:165
  61.2 49.2 %all-to-all-start.1 = ((bf16[16,48,1280]{2,1,0:T(8,128)(2,1)}), bf16[16,48,1280]{2,1,0:T(8,128)(2,1)S(1)}, u32[]{:S(2)}, u32[]{:S(2)}) async-start(bf16[16,48,1280]{2,1,0:T(8,128)(2,1)} %bitcast.44), calls=%async_computation.1 | async-start | bytes 3932160 | tf_op jit(solution)/shard_map/all_to_all | solution.py:263
  69.9 33.8 %collective-permute-start.2 = (bf16[384,1920]{1,0:T(8,128)(2,1)}, bf16[384,1920]{1,0:T(8,128)(2,1)}, u32[]{:S(2)}, u32[]{:S(2)}) collective-permute-start(bf16[384,1920]{1,0:T(8,128)(2,1)} %multiply_convert_fusion.5), channel_id=1, source_target_pairs={{0,1},{1,0},{2,3},{3,2},{4,5},{5,4},{6,7},{7,6},{8,9},{9,8},{10,11... | collective-permute-start | bytes 4423688 | tf_op jit(solution)/shard_map/ppermute | solution.py:165
  75.8 6.9 %copy-start.11 = (f32[384,1024]{1,0:T(8,128)S(1)}, f32[384,1024]{1,0:T(8,128)}, u32[]{:S(2)}) copy-start(f32[384,1024]{1,0:T(8,128)} %fusion.6) | copy-start | bytes 4718596
  82.7 21.0 %copy-start.17 = (bf16[768,1920]{1,0:T(8,128)(2,1)S(1)}, bf16[768,1920]{1,0:T(8,128)(2,1)}, u32[]{:S(2)}) copy-start(bf16[768,1920]{1,0:T(8,128)(2,1)} %convolution_convert_fusion.1) | copy-start | bytes 8847364
  111.7 69.8 %all-to-all-start = ((bf16[16,48,1920]{2,1,0:T(8,128)(2,1)}), bf16[16,48,1920]{2,1,0:T(8,128)(2,1)S(1)}, u32[]{:S(2)}, u32[]{:S(2)}) async-start(bf16[16,48,1920]{2,1,0:T(8,128)(2,1)} %bitcast.42), calls=%async_computation | async-start | bytes 5898240 | tf_op jit(solution)/shard_map/all_to_all | solution.py:263
  121.5 57.0 %collective-permute-start.4 = (bf16[384,3328]{1,0:T(8,128)(2,1)}, bf16[384,3328]{1,0:T(8,128)(2,1)}, u32[]{:S(2)}, u32[]{:S(2)}) collective-permute-start(bf16[384,3328]{1,0:T(8,128)(2,1)} %multiply_convert_fusion.1), channel_id=1, source_target_pairs={{0,1},{1,0},{2,3},{3,2},{4,5},{5,4},{6,7},{7,6},{8,9},{9,8},{10,11... | collective-permute-start | bytes 7667720 | tf_op jit(solution)/shard_map/ppermute | solution.py:165
  131.2 47.3 %collective-permute-start.3 = (f32[384]{0:T(512)S(1)}, f32[384]{0:T(512)S(1)}, u32[]{:S(2)}, u32[]{:S(2)}) collective-permute-start(f32[384]{0:T(512)S(1)} %add_rsqrt_fusion), channel_id=1, source_target_pairs={{0,1},{1,0},{2,3},{3,2},{4,5},{5,4},{6,7},{7,6},{8,9},{9,8},{10,11... | collective-permute-start | bytes 4616 | tf_op jit(solution)/shard_map/ppermute | solution.py:165
  137.2 5.8 %copy-start.12 = (bf16[8,4096,64]{1,2,0:T(8,128)(2,1)S(1)}, bf16[8,4096,64]{1,2,0:T(8,128)(2,1)}, u32[]{:S(2)}) copy-start(bf16[8,4096,64]{1,2,0:T(8,128)(2,1)} %param.9) | copy-start | bytes 12582916
  187.6 5.6 %collective-permute-start.5 = (f32[64,768]{1,0:T(8,128)S(1)}, f32[64,768]{1,0:T(8,128)S(1)}, u32[]{:S(2)}, u32[]{:S(2)}) collective-permute-start(f32[64,768]{1,0:T(8,128)S(1)} %shard_map.64), channel_id=1, source_target_pairs={{0,1},{1,0},{2,3},{3,2},{4,5},{5,4},{6,7},{7,6},{8,9},{9,8},{10,11... | collective-permute-start | bytes 589832 | tf_op jit(solution)/shard_map/ppermute | solution.py:165
  194.4 23.5 %collective-permute-start.6 = (bf16[384,768]{1,0:T(8,128)(2,1)S(1)}, bf16[384,768]{1,0:T(8,128)(2,1)}, u32[]{:S(2)}, u32[]{:S(2)}) collective-permute-start(bf16[384,768]{1,0:T(8,128)(2,1)S(1)} %multiply_convert_fusion.14), channel_id=1, source_target_pairs={{0,1},{1,0},{2,3},{3,2},{4,5},{5,4},{6,7},{7,6},{8,9},{9,8},{10,11... | collective-permute-start | bytes 1769480 | tf_op jit(solution)/shard_map/ppermute | solution.py:165
  197.2 28.4 %all-to-all-start.4 = ((bf16[16,48,512]{2,1,0:T(8,128)(2,1)}), bf16[16,48,512]{2,1,0:T(8,128)(2,1)S(1)}, u32[]{:S(2)}, u32[]{:S(2)}) async-start(bf16[16,48,512]{2,1,0:T(8,128)(2,1)} %bitcast.19), calls=%async_computation.4 | async-start | bytes 1572864 | tf_op jit(solution)/shard_map/all_to_all | solution.py:309
  206.0 4.6 %copy-start.7 = (f32[384,1024]{1,0:T(8,128)S(1)}, f32[384,1024]{1,0:T(8,128)}, u32[]{:S(2)}) copy-start(f32[384,1024]{1,0:T(8,128)} %add.227) | copy-start | bytes 4718596
  212.0 5.9 %copy-start.8 = (f32[384,1024]{1,0:T(8,128)S(1)}, f32[384,1024]{1,0:T(8,128)}, u32[]{:S(2)}) copy-start(f32[384,1024]{1,0:T(8,128)} %add_add_fusion.1) | copy-start | bytes 4718596
  217.8 7.7 %copy-start.4 = (s32[384,1]{1,0:T(8,128)S(1)}, s32[384,1]{1,0:T(8,128)}, u32[]{:S(2)}) copy-start(s32[384,1]{1,0:T(8,128)} %broadcast_in_dim.75.refs_0_) | copy-start | bytes 4612
  217.8 7.7 %copy-start.5 = (s32[384,1]{1,0:T(8,128)S(1)}, s32[384,1]{1,0:T(8,128)}, u32[]{:S(2)}) copy-start(s32[384,1]{1,0:T(8,128)} %broadcast_in_dim.76.refs_1_) | copy-start | bytes 4612
  (8 other events, 13.2 us)
